TPU v7x, 128 devices: a whole 4x4x4 slice. The times are simulated.
128 devices in a mesh: leaf: 2 (over core), prow: 2 (over x_hi), pcol: 32 (over z, y, x_lo).
Axes of the slice: x: 4 (x_hi: 2, x_lo: 2; x = x_hi * 2 + x_lo), y: 4, z: 4, core: 2. Of those that a mesh axis runs over, the one named last changes fastest.
Arguments:
- known_above: bfloat16 [2, 2, 256, 256], P('prow'), may hold values from -6 to 6
- seed_top: float32 [2, 2, 32, 2, 256, 256], P('leaf', 'prow', 'pcol'), may hold values from -6 to 6
- seed_mid: float32 [2, 2, 32, 2, 256, 256], P('leaf', 'prow', 'pcol'), may hold values from -6 to 6
- seed_low: float32 [2, 2, 32, 2, 256, 256], P('leaf', 'prow', 'pcol'), may hold values from -6 to 6
- inverse_top: bfloat16 [2, 2, 32, 2, 256, 256], P('leaf', 'prow', 'pcol'), may hold values from -0.375 to 0.375
- middle_inverses: bfloat16 [2, 2, 32, 2, 256, 256], P('leaf', 'prow', 'pcol'), may hold values from -0.375 to 0.375
- inverse_low: bfloat16 [2, 2, 32, 2, 256, 256], P('leaf', 'prow', 'pcol'), may hold values from -0.375 to 0.375
- tiles_top: bfloat16 [2, 2, 32, 58, 256, 256], P('leaf', 'prow', 'pcol'), may hold values from -0.046875 to 0.046875
- tiles_mid: bfloat16 [2, 2, 32, 58, 256, 256], P('leaf', 'prow', 'pcol'), may hold values from -0.046875 to 0.046875
- tiles_low: bfloat16 [2, 2, 32, 58, 256, 256], P('leaf', 'prow', 'pcol'), may hold values from -0.046875 to 0.046875
- top_source_rows: int32 [2, 2, 32, 58], P('leaf', 'prow', 'pcol'), may hold values from 0 to 1
- source_mid: int32 [2, 2, 32, 58], P('leaf', 'prow', 'pcol'), may hold values from 0 to 129
- lowest_source_rows: int32 [2, 2, 32, 58], P('leaf', 'prow', 'pcol'), may hold values from 0 to 193
- target_top: int32 [2, 2, 32, 58], P('leaf', 'prow', 'pcol'), may hold values from 0 to 3
- target_mid: int32 [2, 2, 32, 58], P('leaf', 'prow', 'pcol'), may hold values from 0 to 3
- target_low: int32 [2, 2, 32, 58], P('leaf', 'prow', 'pcol'), may hold values from 0 to 3
Outputs:
- solved_top: float32 [2, 2, 32, 2, 256, 256], P('leaf', 'prow', 'pcol')
- solved_mid: float32 [2, 2, 32, 2, 256, 256], P('leaf', 'prow', 'pcol')
- solved_low: float32 [2, 2, 32, 2, 256, 256], P('leaf', 'prow', 'pcol')
All inputs are finite; a program needn't handle non-finite values.
Results may differ from a plain program's by a relative error of at most 0.015.
Values may be sent and summed in bfloat16 or wider, within the bound.
No kernel may reach another device: no remote copies, remote signals or barrier semaphores. Data moves between devices by JAX's collectives and lax.ppermute only.
A program may use at most 192 MiB of HBM per device.

v0:
```python
import jax
import jax.numpy as jnp
from jax import lax
from jax.sharding import PartitionSpec as P


def level_pass(row_store, tiles, source, target, right_side, inverse):
    per_dev = right_side.shape[0]
    columns = lax.axis_size("prow") * per_dev
    picked = jnp.take(row_store, source[0, 0, 0], axis=0)
    products = jnp.einsum(
        "tra,tab->trb", picked, tiles[0, 0, 0], preferred_element_type=jnp.float32
    )
    choice_mask = (
        target[0, 0, 0][None, :] == jnp.arange(columns, dtype=jnp.int32)[:, None]
    ).astype(jnp.bfloat16)
    upper_portion = products.astype(jnp.bfloat16)
    lower_portion = (products - upper_portion.astype(jnp.float32)).astype(jnp.bfloat16)
    partial_value = jnp.einsum(
        "qk,kzx->qzx", choice_mask, upper_portion, preferred_element_type=jnp.float32
    )
    partial_value = partial_value + jnp.einsum(
        "qk,kzx->qzx", choice_mask, lower_portion, preferred_element_type=jnp.float32
    )
    column_sums = lax.psum_scatter(
        partial_value.astype(jnp.bfloat16), "prow", scatter_dimension=0, tiled=True
    ).astype(jnp.float32)
    reduced = (right_side - column_sums).astype(jnp.bfloat16)
    return jnp.einsum("drb,dab->dra", reduced, inverse[0, 0, 0], preferred_element_type=jnp.float32)


def collect_shared(rounded):
    return lax.all_gather(rounded, ("leaf", "pcol"), axis=0, tiled=True)


def collect_own(rounded):
    return lax.all_gather(rounded, "pcol", axis=0, tiled=True)


def window(known_above, right_sides, inverses, tiles, sources, targets):
    row_store = known_above[0]
    results = []
    for level in range(3):
        right_side = right_sides[level][0, 0, 0]
        solved_state = level_pass(
            row_store, tiles[level], sources[level], targets[level], right_side, inverses[level]
        )
        results.append(solved_state)
        if level == 0:
            row_store = jnp.concatenate(
                [row_store, collect_shared(solved_state.astype(jnp.bfloat16))], axis=0
            )
        elif level == 1:
            row_store = jnp.concatenate(
                [row_store, collect_own(solved_state.astype(jnp.bfloat16))], axis=0
            )
    return results


def local(
    known_above,
    seed_top,
    seed_mid,
    seed_low,
    inverse_top,
    middle_inverses,
    inverse_low,
    tiles_top,
    tiles_mid,
    tiles_low,
    top_source_rows,
    source_mid,
    lowest_source_rows,
    target_top,
    target_mid,
    target_low,
):
    right_sides = (seed_top, seed_mid, seed_low)
    inverses = (inverse_top, middle_inverses, inverse_low)
    tiles = (tiles_top, tiles_mid, tiles_low)
    sources = (top_source_rows, source_mid, lowest_source_rows)
    targets = (target_top, target_mid, target_low)
    pieces = [window(known_above, right_sides, inverses, tiles, sources, targets)]
    outputs = []
    for level in range(3):
        joined = jnp.concatenate([piece[level] for piece in pieces], axis=1)
        outputs.append(joined[None, None, None])
    return (outputs[0], outputs[1], outputs[2])


def solution(mesh):
    in_specs = (
        P("prow", None, None, None),
        P("leaf", "prow", "pcol", None, None, None),
        P("leaf", "prow", "pcol", None, None, None),
        P("leaf", "prow", "pcol", None, None, None),
        P("leaf", "prow", "pcol", None, None, None),
        P("leaf", "prow", "pcol", None, None, None),
        P("leaf", "prow", "pcol", None, None, None),
        P("leaf", "prow", "pcol", None, None, None),
        P("leaf", "prow", "pcol", None, None, None),
        P("leaf", "prow", "pcol", None, None, None),
        P("leaf", "prow", "pcol", None),
        P("leaf", "prow", "pcol", None),
        P("leaf", "prow", "pcol", None),
        P("leaf", "prow", "pcol", None),
        P("leaf", "prow", "pcol", None),
        P("leaf", "prow", "pcol", None),
    )
    out_specs = (
        P("leaf", "prow", "pcol", None, None, None),
        P("leaf", "prow", "pcol", None, None, None),
        P("leaf", "prow", "pcol", None, None, None),
    )
    return jax.shard_map(local, mesh=mesh, in_specs=in_specs, out_specs=out_specs, check_vma=False)
```

profile of v0, /device:TPU:10, one launch (start us, length us, event | category | flops | bytes accessed | tf_op | source)
XLA Modules:
  0.0 544.9 jit_solution(271164094548625428)
XLA Ops:
  7.2 0.0 reduce-scatter.4.cloned.1.call-start
  7.2 0.7 fusion.56
  7.9 0.7 compare_and_fusion.2
  8.6 6.1 %gather_fusion = bf16[58,256,256]{2,1,0:T(8,128)(2,1)} fusion(bf16[2,256,256]{2,1,0:T(8,128)(2,1)} %bitcast.85, s32[1024]{0:T(1024)S(1)} %pad_clamp_fusion.2), kind=kCustom, calls=%fused_computation | custom fusion | bytes 15204584 | tf_op jit(solution)/shard_map/jit(_take)/gather | solution.py:10
  14.7 12.9 %subtract_convert_fusion.2 = (bf16[58,256,256]{2,1,0:T(8,128)(2,1)}, bf16[58,256,256]{2,1,0:T(8,128)(2,1)}) fusion(bf16[1,1,1,58,256,256]{5,4,3,2,1,0:T(8,128)(2,1)} %param.23, bf16[58,256,256]{2,1,0:T(8,128)(2,1)} %gather_fusion, pred[58]{0:T(512)(128)(4,1)S(1)} %compare_and_fusion.2), kind=kOutput, calls=%fused_computation.7 | convolution fusion | flops 1965162496 | bytes 30408762 | tf_op jit(solution)/shard_map/tra,tab->trb/dot_general | solution.py:11
  27.6 7.5 %fusion.8 = f32[4,256,256]{2,0,1:T(4,128)S(1)} fusion(bf16[58,256,256]{2,1,0:T(8,128)(2,1)} %get-tuple-element.7, s32[58]{0:T(128)S(1)} %bitcast.90), kind=kOutput, calls=%fused_computation.16 | convolution fusion | flops 30408936 | bytes 8650984 | tf_op jit(solution)/shard_map/qk,kzx->qzx/dot_general | solution.py:22
  35.1 4.2 fusion.10
  39.3 1.1 fusion.29
  40.4 0.0 all-gather.3.cloned.1.call-start
  40.5 20.0 %reduce-scatter.4.cloned.1.call-done = bf16[2,256,256]{2,1,0:T(8,128)(2,1)} async-done(((bf16[4,256,256]{2,1,0:T(8,128)(2,1)}), bf16[2,256,256]{2,1,0:T(8,128)(2,1)}) %reduce-scatter.4.cloned.1.call-update) | async-done | bytes 262160 | tf_op jit(solution)/shard_map/reduce_scatter | solution.py:25
  60.4 2.1 fusion.62
  62.6 0.0 reduce-scatter.6.cloned.1.call-start
  62.7 123.3 %all-gather.3.cloned.1.call-done = bf16[128,256,256]{2,1,0:T(8,128)(2,1)} async-done(((bf16[2,256,256]{2,1,0:T(8,128)(2,1)}), bf16[128,256,256]{2,1,0:T(8,128)(2,1)}) %all-gather.3.cloned.1.call-update) | async-done | bytes 16777232 | tf_op jit(solution)/shard_map/all_gather | solution.py:33
  186.0 14.3 %pad_maximum_fusion.1 = bf16[130,256,256]{2,1,0:T(8,128)(2,1)} fusion(bf16[128,256,256]{2,1,0:T(8,128)(2,1)} %all-gather.3.cloned.1.call-done, bf16[2,256,256]{2,1,0:T(8,128)(2,1)S(1)} %bitcast.86), kind=kLoop, calls=%fused_computation.4 | loop fusion | flops 8519680 | bytes 34078720 | tf_op jit(solution)/shard_map/concatenate | solution.py:50
  200.3 11.1 %gather_fusion.1 = bf16[58,256,256]{2,1,0:T(8,128)(2,1)} fusion(bf16[130,256,256]{2,1,0:T(8,128)(2,1)} %pad_maximum_fusion.1, s32[1024]{0:T(1024)S(1)} %pad_clamp_fusion.1), kind=kCustom, calls=%fused_computation.1 | custom fusion | bytes 15204584 | tf_op jit(solution)/shard_map/jit(_take)/gather | solution.py:10
  211.4 12.8 %subtract_convert_fusion.1 = (bf16[58,256,256]{2,1,0:T(8,128)(2,1)}, bf16[58,256,256]{2,1,0:T(8,128)(2,1)}) fusion(bf16[1,1,1,58,256,256]{5,4,3,2,1,0:T(8,128)(2,1)} %param.24, bf16[58,256,256]{2,1,0:T(8,128)(2,1)} %gather_fusion.1, pred[58]{0:T(512)(128)(4,1)S(1)} %compare_and_fusion.1), kind=kOutput, calls=%fused_computation.6 | convolution fusion | flops 1965162496 | bytes 30408762 | tf_op jit(solution)/shard_map/tra,tab->trb/dot_general | solution.py:11
  224.2 7.5 %fusion.4 = f32[4,256,256]{2,0,1:T(4,128)S(1)} fusion(bf16[58,256,256]{2,1,0:T(8,128)(2,1)} %get-tuple-element.5, s32[58]{0:T(128)S(1)} %bitcast.92), kind=kOutput, calls=%fused_computation.12 | convolution fusion | flops 30408936 | bytes 8650984 | tf_op jit(solution)/shard_map/qk,kzx->qzx/dot_general | solution.py:22
  231.7 4.2 fusion.6
  235.9 1.1 fusion.28
  237.0 0.0 all-gather.5.cloned.1.call-start
  237.1 17.4 %reduce-scatter.6.cloned.1.call-done = bf16[2,256,256]{2,1,0:T(8,128)(2,1)} async-done(((bf16[4,256,256]{2,1,0:T(8,128)(2,1)}), bf16[2,256,256]{2,1,0:T(8,128)(2,1)}) %reduce-scatter.6.cloned.1.call-update) | async-done | bytes 262160 | tf_op jit(solution)/shard_map/reduce_scatter | solution.py:25
  254.5 2.1 fusion.63
  256.6 0.0 reduce-scatter.8.cloned.1.call-start
  256.7 186.6 %all-gather.5.cloned.1.call-done = bf16[64,256,256]{2,1,0:T(8,128)(2,1)} async-done(((bf16[2,256,256]{2,1,0:T(8,128)(2,1)}), bf16[64,256,256]{2,1,0:T(8,128)(2,1)}) %all-gather.5.cloned.1.call-update) | async-done | bytes 8388624 | tf_op jit(solution)/shard_map/all_gather | solution.py:37
  443.3 34.2 %pad_maximum_fusion = bf16[194,256,256]{2,1,0:T(8,128)(2,1)} fusion(bf16[64,256,256]{2,1,0:T(8,128)(2,1)} %all-gather.5.cloned.1.call-done, bf16[128,256,256]{2,1,0:T(8,128)(2,1)} %all-gather.3.cloned.1.call-done, bf16[2,256,256]{2,1,0:T(8,128)(2,1)S(1)} %bitcast.87), kind=kLoop, calls=%fused_computation.3 | loop fusion | flops 25427968 | bytes 50855936 | tf_op jit(solution)/shard_map/concatenate | solution.py:54
  477.5 13.5 %gather_fusion.2 = bf16[58,256,256]{2,1,0:T(8,128)(2,1)} fusion(bf16[194,256,256]{2,1,0:T(8,128)(2,1)} %pad_maximum_fusion, s32[1024]{0:T(1024)S(1)} %pad_clamp_fusion), kind=kCustom, calls=%fused_computation.2 | custom fusion | bytes 15204584 | tf_op jit(solution)/shard_map/jit(_take)/gather | solution.py:10
  491.0 12.8 %subtract_convert_fusion = (bf16[58,256,256]{2,1,0:T(8,128)(2,1)}, bf16[58,256,256]{2,1,0:T(8,128)(2,1)}) fusion(bf16[1,1,1,58,256,256]{5,4,3,2,1,0:T(8,128)(2,1)} %param.25, bf16[58,256,256]{2,1,0:T(8,128)(2,1)} %gather_fusion.2, pred[58]{0:T(512)(128)(4,1)S(1)} %compare_and_fusion), kind=kOutput, calls=%fused_computation.5 | convolution fusion | flops 1965162496 | bytes 30408762 | tf_op jit(solution)/shard_map/tra,tab->trb/dot_general | solution.py:11
  503.8 7.5 %fusion = f32[4,256,256]{2,0,1:T(4,128)S(1)} fusion(bf16[58,256,256]{2,1,0:T(8,128)(2,1)} %get-tuple-element.3, s32[58]{0:T(128)S(1)} %bitcast.94), kind=kOutput, calls=%fused_computation.8 | convolution fusion | flops 30408936 | bytes 8650984 | tf_op jit(solution)/shard_map/qk,kzx->qzx/dot_general | solution.py:22
  511.3 4.2 fusion.2
  515.5 1.1 fusion.27
  516.6 19.6 %reduce-scatter.8.cloned.1.call-done = bf16[2,256,256]{2,1,0:T(8,128)(2,1)} async-done(((bf16[4,256,256]{2,1,0:T(8,128)(2,1)}), bf16[2,256,256]{2,1,0:T(8,128)(2,1)}) %reduce-scatter.8.cloned.1.call-update) | async-done | bytes 262160 | tf_op jit(solution)/shard_map/reduce_scatter | solution.py:25
  536.2 2.0 convolution_bitcast_fusion
  (44 shorter events, 0.2 us)
Async XLA Ops:
  7.2 53.3 %copy-start = (bf16[1,1,1,2,256,256]{5,4,3,2,1,0:T(8,128)(2,1)S(1)}, bf16[1,1,1,2,256,256]{5,4,3,2,1,0:T(8,128)(2,1)}, u32[]{:S(2)}) copy-start(bf16[1,1,1,2,256,256]{5,4,3,2,1,0:T(8,128)(2,1)} %param.20) | copy-start | bytes 786436
  7.2 53.3 %reduce-scatter.4.cloned.1.call-start = ((), (), s32[]{:S(2)}) async-start(), calls=%async_computation.3 | async-start | bytes 786432 | tf_op jit(solution)/shard_map/reduce_scatter | solution.py:25
  14.7 12.9 %copy-start.11 = (s32[1,1,1,58]{3,2,1,0:T(1,128)S(1)}, s32[1,1,1,58]{3,2,1,0:T(1,128)}, u32[]{:S(2)}) copy-start(s32[1,1,1,58]{3,2,1,0:T(1,128)} %param.29) | copy-start | bytes 700
  27.6 7.5 %copy-start.3 = (bf16[58,256,256]{2,1,0:T(8,128)(2,1)S(1)}, bf16[58,256,256]{2,1,0:T(8,128)(2,1)}, u32[]{:S(2)}) copy-start(bf16[58,256,256]{2,1,0:T(8,128)(2,1)} %get-tuple-element.8) | copy-start | bytes 22806532
  35.1 25.3 %copy-start.6 = (f32[1,1,1,2,256,256]{5,4,3,2,1,0:T(8,128)S(1)}, f32[1,1,1,2,256,256]{5,4,3,2,1,0:T(8,128)}, u32[]{:S(2)}) copy-start(f32[1,1,1,2,256,256]{5,4,3,2,1,0:T(8,128)} %param.17) | copy-start | bytes 1572868
  35.1 27.5 %copy-start.14 = (s32[1,1,1,58]{3,2,1,0:T(1,128)S(1)}, s32[1,1,1,58]{3,2,1,0:T(1,128)}, u32[]{:S(2)}) copy-start(s32[1,1,1,58]{3,2,1,0:T(1,128)} %param.27) | copy-start | bytes 700
  35.1 150.9 %copy-start.2 = (bf16[1,2,256,256]{3,2,1,0:T(8,128)(2,1)S(1)}, bf16[1,2,256,256]{3,2,1,0:T(8,128)(2,1)}, u32[]{:S(2)}) copy-start(bf16[1,2,256,256]{3,2,1,0:T(8,128)(2,1)} %param.16) | copy-start | bytes 786436
  40.4 145.6 %all-gather.3.cloned.1.call-start = ((), (), s32[]{:S(2)}) async-start(), calls=%async_computation.4 | async-start | bytes 17039360 | tf_op jit(solution)/shard_map/all_gather | solution.py:33
  62.6 191.9 %reduce-scatter.6.cloned.1.call-start = ((), (), s32[]{:S(2)}) async-start(), calls=%async_computation.5 | async-start | bytes 786432 | tf_op jit(solution)/shard_map/reduce_scatter | solution.py:25
  211.4 12.8 %copy-start.12 = (s32[1,1,1,58]{3,2,1,0:T(1,128)S(1)}, s32[1,1,1,58]{3,2,1,0:T(1,128)}, u32[]{:S(2)}) copy-start(s32[1,1,1,58]{3,2,1,0:T(1,128)} %param.30) | copy-start | bytes 700
  224.2 7.5 %copy-start.4 = (bf16[58,256,256]{2,1,0:T(8,128)(2,1)S(1)}, bf16[58,256,256]{2,1,0:T(8,128)(2,1)}, u32[]{:S(2)}) copy-start(bf16[58,256,256]{2,1,0:T(8,128)(2,1)} %get-tuple-element.6) | copy-start | bytes 22806532
  231.7 22.8 %copy-start.7 = (f32[1,1,1,2,256,256]{5,4,3,2,1,0:T(8,128)S(1)}, f32[1,1,1,2,256,256]{5,4,3,2,1,0:T(8,128)}, u32[]{:S(2)}) copy-start(f32[1,1,1,2,256,256]{5,4,3,2,1,0:T(8,128)} %param.18) | copy-start | bytes 1572868
  231.7 22.8 %copy-start.9 = (bf16[1,1,1,2,256,256]{5,4,3,2,1,0:T(8,128)(2,1)S(1)}, bf16[1,1,1,2,256,256]{5,4,3,2,1,0:T(8,128)(2,1)}, u32[]{:S(2)}) copy-start(bf16[1,1,1,2,256,256]{5,4,3,2,1,0:T(8,128)(2,1)} %param.21) | copy-start | bytes 786436
  231.7 24.9 %copy-start.15 = (s32[1,1,1,58]{3,2,1,0:T(1,128)S(1)}, s32[1,1,1,58]{3,2,1,0:T(1,128)}, u32[]{:S(2)}) copy-start(s32[1,1,1,58]{3,2,1,0:T(1,128)} %param.28) | copy-start | bytes 700
  237.0 206.3 %all-gather.5.cloned.1.call-start = ((), (), s32[]{:S(2)}) async-start(), calls=%async_computation.6 | async-start | bytes 8650752 | tf_op jit(solution)/shard_map/all_gather | solution.py:37
  256.6 279.6 %reduce-scatter.8.cloned.1.call-start = ((), (), s32[]{:S(2)}) async-start(), calls=%async_computation.7 | async-start | bytes 786432 | tf_op jit(solution)/shard_map/reduce_scatter | solution.py:25
  491.0 12.8 %copy-start.13 = (s32[1,1,1,58]{3,2,1,0:T(1,128)S(1)}, s32[1,1,1,58]{3,2,1,0:T(1,128)}, u32[]{:S(2)}) copy-start(s32[1,1,1,58]{3,2,1,0:T(1,128)} %param.31) | copy-start | bytes 700
  503.8 7.5 %copy-start.5 = (bf16[58,256,256]{2,1,0:T(8,128)(2,1)S(1)}, bf16[58,256,256]{2,1,0:T(8,128)(2,1)}, u32[]{:S(2)}) copy-start(bf16[58,256,256]{2,1,0:T(8,128)(2,1)} %get-tuple-element.4) | copy-start | bytes 22806532
  503.8 34.4 %copy-start.1 = (bf16[1,1,1,2,256,256]{5,4,3,2,1,0:T(8,128)(2,1)S(1)}, bf16[1,1,1,2,256,256]{5,4,3,2,1,0:T(8,128)(2,1)}, u32[]{:S(2)}) copy-start(bf16[1,1,1,2,256,256]{5,4,3,2,1,0:T(8,128)(2,1)} %param.20) | copy-start | bytes 786436
  511.3 24.9 %copy-start.8 = (f32[1,1,1,2,256,256]{5,4,3,2,1,0:T(8,128)S(1)}, f32[1,1,1,2,256,256]{5,4,3,2,1,0:T(8,128)}, u32[]{:S(2)}) copy-start(f32[1,1,1,2,256,256]{5,4,3,2,1,0:T(8,128)} %param.19) | copy-start | bytes 1572868
  511.3 24.9 %copy-start.10 = (bf16[1,1,1,2,256,256]{5,4,3,2,1,0:T(8,128)(2,1)S(1)}, bf16[1,1,1,2,256,256]{5,4,3,2,1,0:T(8,128)(2,1)}, u32[]{:S(2)}) copy-start(bf16[1,1,1,2,256,256]{5,4,3,2,1,0:T(8,128)(2,1)} %param.22) | copy-start | bytes 786436
Sparse Core Ops, SparseCore 0:
  40.5 19.8 reduce-scatter.3
  62.8 123.0 all-gather.2
  237.1 17.2 reduce-scatter.5
  256.7 186.5 all-gather.4
  516.7 19.4 reduce-scatter.7
where the time goes:
time: 552 us; the launch traced here: 545 us
  waiting for transfers between devices  367 us (66%)
  matrix products  79.7 us (14%)
  other arithmetic  53.1 us (10%)
  local copies, waits for them, and re-layouts  30.8 us (6%)
  between operations  14.1 us (3%)
    all_gather x1, waiting for transfers between devices, collect_own(): return lax.all_gather(rounded, 'pcol', axis=0, tiled=True)  187 us
    all_gather x1, waiting for transfers between devices, collect_shared(): return lax.all_gather(rounded, ('leaf', 'pcol'), axis=0, tiled=True)  123 us
    reduce_scatter x3, waiting for transfers between devices, level_pass(): lax.psum_scatter(partial_value.astype(jnp.bfloat16), 'prow', scatter_dime...  57 us
    dot_general x3, matrix products, level_pass(): jnp.einsum('tra,tab->trb', picked, tiles[0, 0, 0], preferred_element_type...  38.5 us
    concatenate x1, other arithmetic, window(): jnp.concatenate([row_store, collect_own(solved_state.astype(jnp.bfloat16)...  34.2 us
    gather x3, local copies, waits for them, and re-layouts, level_pass(): picked = jnp.take(row_store, source[0, 0, 0], axis=0)  30.8 us
    dot_general x3, matrix products, level_pass(): jnp.einsum('qk,kzx->qzx', choice_mask, lower_portion, preferred_element_t...  22.5 us
    concatenate x1, other arithmetic, window(): jnp.concatenate([row_store, collect_shared(solved_state.astype(jnp.bfloat...  14.3 us
  transfers between devices with their start and end apart: 5, of which 5 were waited for; matrix products, arithmetic and copies ran while one was open for 0% of the time, Pallas kernels for 0%

commit v1 on v0

v1 whole, which is shorter than its diff:
```python
import functools

import jax
import jax.numpy as jnp
from jax import lax
from jax.experimental import pallas as pl
from jax.experimental.pallas import tpu as pltpu
from jax.sharding import PartitionSpec as P

BF16 = jnp.bfloat16
F32 = jnp.float32


def products_kernel(columns, stores_of, with_init, *refs):
    order, loc, starts = refs[:3]
    n_stores = 1 + max(store for _, store in stores_of)
    stores = refs[3 : 3 + n_stores]
    refs = refs[3 + n_stores :]
    tiles, refs = refs[0], refs[1:]
    if with_init:
        init, refs = refs[0], refs[1:]
    out, row_buf, tile_buf, acc, sem = refs
    depth = tiles.shape[1]

    def at(i, n=1):
        return pl.ds(pl.multiple_of(i * depth, depth), n * depth)

    def row_copy(store, i):
        return pltpu.make_async_copy(stores[store].at[loc[i]], row_buf.at[:, at(i)], sem.at[i])

    def tile_copy(i):
        return pltpu.make_async_copy(tiles.at[order[i]], tile_buf.at[at(i)], sem.at[i])

    for base in columns:
        for group, store in stores_of:

            def issue(i, carry, store=store):
                tile_copy(i).start()
                row_copy(store, i).start()
                return carry

            lax.fori_loop(starts[base + group], starts[base + group + 1], issue, 0)

    if with_init:
        acc[...] = init[...]
    else:
        acc[...] = jnp.zeros_like(acc)

    for c, base in enumerate(columns):
        first = starts[base + stores_of[0][0]]
        last = starts[base + stores_of[-1][0] + 1]

        def multiply(i, n, c=c):
            for k in range(n):
                both = tile_buf.at[pl.ds(0, depth + row_buf.shape[0])]
                pltpu.make_async_copy(both, both, sem.at[i + k]).wait()
            acc[c] += jnp.dot(row_buf[:, at(i, n)], tile_buf[at(i, n)], preferred_element_type=F32)

        def several(j, carry, first=first, multiply=multiply):
            multiply(first + RUN * j, RUN)
            return carry

        runs = (last - first) // RUN
        lax.fori_loop(0, runs, several, 0)
        first = first + runs * RUN
        size = RUN // 2
        while size:

            def rest(j, carry, first=first, size=size, multiply=multiply):
                multiply(first, size)
                return carry

            some = (last - first) // size
            lax.fori_loop(0, some, rest, 0)
            first = first + some * size
            size //= 2
    out[...] = acc[...].astype(out.dtype)


RUN = 4


def tile_products(index, columns, stores_of, stores, tiles, out_dtype, init=None):
    order, loc, starts = index
    count, depth, width = tiles.shape
    rows = stores[0].shape[1]
    in_hbm = pl.BlockSpec(memory_space=pltpu.HBM)
    in_vmem = pl.BlockSpec(memory_space=pltpu.VMEM)
    in_smem = pl.BlockSpec(memory_space=pltpu.SMEM)
    operands = [order, loc, starts, *stores, tiles]
    specs = [in_smem] * 3 + [in_hbm] * (len(stores) + 1)
    if init is not None:
        operands.append(init)
        specs.append(in_vmem)
    return pl.pallas_call(
        functools.partial(products_kernel, tuple(columns), tuple(stores_of), init is not None),
        out_shape=jax.ShapeDtypeStruct((len(columns), rows, width), out_dtype),
        in_specs=specs,
        out_specs=in_vmem,
        scratch_shapes=[
            pltpu.VMEM((rows, count * depth), BF16),
            pltpu.VMEM((count * depth, width), BF16),
            pltpu.VMEM((len(columns), rows, width), F32),
            pltpu.SemaphoreType.DMA((count,)),
        ],
        compiler_params=pltpu.CompilerParams(vmem_limit_bytes=60 * 1024 * 1024),
        cost_estimate=pl.CostEstimate(
            flops=count * rows * depth * width, bytes_accessed=count * depth * width * 2, transcendentals=0
        ),
    )(*operands)


def top_kernel(per_dev, row, source, target, known, tiles, away, mine, tile_buf, total, tile_sem):
    count = tiles.shape[0]
    upper, depth = known.shape[0], known.shape[2]

    def tile_copy(i):
        return pltpu.make_async_copy(tiles.at[i], tile_buf.at[i], tile_sem.at[i])

    for i in range(count):
        tile_copy(i).start()
    total[...] = jnp.zeros_like(total)

    def add(i, carry):
        tile_copy(i).wait()
        total[target[i] * upper + source[i]] += tile_buf[i].astype(F32)
        return carry

    lax.fori_loop(0, count, add, 0)
    here = row[0]
    for d in range(per_dev):
        for out, side in ((away, 1 - here), (mine, here)):
            first = (side * per_dev + d) * upper
            sums = jnp.zeros(out.shape[1:], F32)
            for k in range(upper):
                whole = total[first + k]
                high = whole.astype(BF16)
                low = (whole - high.astype(F32)).astype(BF16)
                sums += jnp.dot(known[k], high, preferred_element_type=F32)
                sums += jnp.dot(known[k], low, preferred_element_type=F32)
            out[d] = sums.astype(BF16)


def top_products(source, target, known, tiles, per_dev):
    count, depth, width = tiles.shape
    rows = known.shape[1]
    in_vmem = pl.BlockSpec(memory_space=pltpu.VMEM)
    in_smem = pl.BlockSpec(memory_space=pltpu.SMEM)
    row = lax.axis_index("prow").astype(jnp.int32)[None]
    return pl.pallas_call(
        functools.partial(top_kernel, per_dev),
        out_shape=[jax.ShapeDtypeStruct((per_dev, rows, width), BF16)] * 2,
        in_specs=[in_smem] * 3 + [in_vmem, pl.BlockSpec(memory_space=pl.ANY)],
        out_specs=[in_vmem] * 2,
        scratch_shapes=[
            pltpu.VMEM((count, depth, width), BF16),
            pltpu.VMEM((2 * per_dev * known.shape[0], depth, width), F32),
            pltpu.SemaphoreType.DMA((count,)),
        ],
        compiler_params=pltpu.CompilerParams(vmem_limit_bytes=60 * 1024 * 1024),
    )(row, source, target, known, tiles)


def solve_kernel(seed, mine, other, inverse, solved, rounded):
    for d in range(seed.shape[0]):
        sums = mine[d].astype(F32) + other[d].astype(F32)
        reduced = (seed[d] - sums).astype(BF16)
        x = lax.dot_general(reduced, inverse[d], (((1,), (1,)), ((), ())), preferred_element_type=F32)
        solved[d] = x
        rounded[d] = x.astype(BF16)


def solve(seed, mine, other, inverse):
    return pl.pallas_call(
        solve_kernel,
        out_shape=(jax.ShapeDtypeStruct(seed.shape, F32), jax.ShapeDtypeStruct(seed.shape, BF16)),
        in_specs=[pl.BlockSpec(memory_space=pltpu.VMEM)] * 4,
        out_specs=(pl.BlockSpec(memory_space=pltpu.VMEM),) * 2,
    )(seed, mine, other, inverse)


def swap(a, axis):
    return lax.ppermute(a, axis, [(0, 1), (1, 0)])


Z, Y, X = 4, 4, 2


def shift(a, **by):
    def at(z, y, x):
        return ((z % Z) * Y + y % Y) * X + x % X

    dz, dy, dx = by.get("z", 0), by.get("y", 0), by.get("x", 0)
    pairs = [(at(z, y, x), at(z + dz, y + dy, x + dx)) for z in range(Z) for y in range(Y) for x in range(X)]
    return lax.ppermute(a, "pcol", pairs)


def gather(rounded, beside=()):
    orders = (("y", "z"), ("z", "y"))
    across = shift(rounded, x=1)
    pairs = [jnp.concatenate([rounded[d : d + 1], across[d : d + 1]]) for d in range(2)]
    near = [[shift(pair, **{first: by}) for by in (1, -1, 2)] for pair, (first, _) in zip(pairs, orders)]
    planes = []
    for pair, others in zip(pairs, near):
        planes.append(jnp.concatenate([pair, *others]))
    planes = lax.optimization_barrier(planes)
    last = [(shift(plane, **{second: 1}), shift(plane, **{second: -1})) for plane, (_, second) in zip(planes, orders)]
    last, beside = lax.optimization_barrier((last, beside))
    half = planes[0].shape[0] // 2
    pieces = []
    for plane, (up, down), (_, second) in zip(planes, last, orders):
        pieces += [plane, up, down, shift(up[:half], **{second: 1}), shift(down[half:], **{second: -1})]
    return pieces, beside


def place_of(source, upper, n_top):
    per_dev = 2
    own = source - upper
    leaf, column, d = own // (n_top // 2), (own % (n_top // 2)) // per_dev, own % per_dev
    group = jnp.where(own >= n_top, 2, (leaf != lax.axis_index("leaf")).astype(jnp.int32))
    me = lax.axis_index("pcol")
    z = (column // (Y * X) - me // (Y * X)) % Z
    y = (column // X - me // X) % Y
    x = (column - me) % X
    first = jnp.where(d == 0, y, z)
    second = jnp.where(d == 0, z, y)
    nth = jnp.where(first == 0, 0, jnp.where(first == 3, 1, jnp.where(first == 1, 2, 3)))
    at = nth * X + x
    high = (second == 2) & (at >= 4)
    piece = jnp.where(second == 0, 0, jnp.where(second == 3, 1, jnp.where(second == 1, 2, jnp.where(high, 4, 3))))
    at = jnp.where(high, at - 4, at)
    piece = 1 + piece + 5 * d + 10 * group
    in_upper = source < upper
    return jnp.where(in_upper, 0, piece), jnp.where(in_upper, source, at)


N_STORES = 31


def plan(source, target, upper, n_top):
    piece, at = place_of(source, upper, n_top)
    key = ((target + 2 * lax.axis_index("prow") + 2) % 4) * N_STORES + piece
    count = source.shape[0]
    ids = jnp.arange(count, dtype=jnp.int32)
    before = (key[None, :] < key[:, None]) | ((key[None, :] == key[:, None]) & (ids[None, :] < ids[:, None]))
    rank = jnp.sum(before.astype(jnp.int32), axis=1)
    hit = (rank[None, :] == ids[:, None]).astype(jnp.int32)
    order, loc = jnp.sum(hit[None] * jnp.stack([ids, at])[:, None, :], axis=2)
    keys = jnp.arange(4 * N_STORES + 1, dtype=jnp.int32)
    starts = jnp.sum((key[None, :] < keys[:, None]).astype(jnp.int32), axis=1)
    return order, loc, starts


def local(
    known_above,
    seed_top,
    seed_mid,
    seed_low,
    inverse_top,
    middle_inverses,
    inverse_low,
    tiles_top,
    tiles_mid,
    tiles_low,
    top_source_rows,
    source_mid,
    lowest_source_rows,
    target_top,
    target_mid,
    target_low,
):
    known = known_above[0]
    seed_top, seed_mid, seed_low, inverse_top, middle_inverses, inverse_low = (
        a[0, 0, 0] for a in (seed_top, seed_mid, seed_low, inverse_top, middle_inverses, inverse_low)
    )
    tiles_top, tiles_mid, tiles_low = (a[0, 0, 0] for a in (tiles_top, tiles_mid, tiles_low))
    top_source, mid_source, low_source, top_target, mid_target, low_target = (
        a[0, 0, 0]
        for a in (top_source_rows, source_mid, lowest_source_rows, target_top, target_mid, target_low)
    )
    upper = known.shape[0]
    per_dev = seed_top.shape[0]
    n_top = lax.axis_size("leaf") * lax.axis_size("pcol") * per_dev

    away_keys, mine_keys = (0, N_STORES), (2 * N_STORES, 3 * N_STORES)

    def level(index, groups, stores, tiles, dtype, init=(None, None)):
        away = tile_products(index, away_keys, groups, stores, tiles, dtype, init[0])
        mine = tile_products(index, mine_keys, groups, stores, tiles, dtype, init[1])
        return away, mine

    away, mine = top_products(top_source, top_target, known, tiles_top, per_dev)
    solved_top, rounded_top = solve(seed_top, mine, swap(away, "prow"), inverse_top)
    rounded_top, mid_source, low_source = lax.optimization_barrier((rounded_top, mid_source, low_source))
    pieces, _ = gather(rounded_top)
    p0, p1 = pieces[:5], pieces[5:]
    whole = [p0[0], p1[0]]
    whole, direct, far = lax.optimization_barrier(
        (whole, (p0[1], p0[2], p1[1], p1[2]), (p0[3], p0[4], p1[3], p1[4]))
    )
    whole, direct, far = ([swap(piece, "leaf") for piece in some] for some in (whole, direct, far))
    swapped = [whole[0], *direct[:2], *far[:2], whole[1], *direct[2:], *far[2:]]
    stores = [known] + pieces + swapped
    early = [(p, p) for p in range(len(stores))]

    index = plan(mid_source, mid_target, upper, n_top)
    away, mine = level(index, early, stores, tiles_mid, BF16)
    solved_mid, rounded_mid = solve(seed_mid, mine, swap(away, "prow"), middle_inverses)

    index = plan(low_source, low_target, upper, n_top)
    init = level(index, early, stores, tiles_low, F32)
    arrived, init = gather(rounded_mid, init)
    late = [(len(stores) + p, p) for p in range(len(arrived))]
    away, mine = level(index, late, arrived, tiles_low, BF16, init)
    solved_low, _ = solve(seed_low, mine, swap(away, "prow"), inverse_low)
    return tuple(a[None, None, None] for a in (solved_top, solved_mid, solved_low))


def solution(mesh):
    whole = P("leaf", "prow", "pcol")
    in_specs = (P("prow"),) + (whole,) * 15
    return jax.shard_map(local, mesh=mesh, in_specs=in_specs, out_specs=(whole,) * 3, check_vma=False)
```

time: 552 us -> 213 us (0.39); the launches traced: 545 us -> 215 us
  waiting for transfers between devices: 367 us -> 91.7 us
  matrix products: 79.7 us -> 0 us
  starting transfers between devices: 0.21 us -> 55 us
  other arithmetic: 53.1 us -> 3.94 us
  Pallas kernels: 0 us -> 45.3 us
  between operations: 14.1 us -> 0.98 us
  local copies, waits for them, and re-layouts: 30.8 us -> 17.9 us
    all_gather x2 -> x0, waiting for transfers between devices: 310 us -> none  [the longest x1 187 us: collect_own(): return lax.all_gather(rounded, 'pcol', axis=0, tiled=True)]
    ppermute x0 -> x43, waiting for transfers between devices: none -> 91.7 us  [the longest x30 70.3 us: shift(): return lax.ppermute(a, 'pcol', pairs)]
    dot_general x12 -> x0, matrix products: 79.7 us -> none  [the longest x3 38.5 us: level_pass(): jnp.einsum('tra,tab->trb', picked, tiles[0, 0, 0], preferred_element_type...]
    reduce_scatter x3 -> x0, waiting for transfers between devices: 57 us -> none  [level_pass(): lax.psum_scatter(partial_value.astype(jnp.bfloat16), 'prow', scatter_dime...]
    ppermute x0 -> x43, starting transfers between devices: none -> 55 us  [the longest x30 49.1 us: shift(): return lax.ppermute(a, 'pcol', pairs)]
    concatenate x2 -> x4, other arithmetic: 48.5 us -> 0.1 us  [gather(): jnp.concatenate([rounded[d:d + 1], across[d:d + 1]])]
    pallas_call x0 -> x10, Pallas kernels: none -> 45.3 us  [the longest x6 31.7 us: tile_products(): pl.pallas_call(functools.partial(products_kernel, tuple(columns), tuple(s...]
    gather x3 -> x0, local copies, waits for them, and re-layouts: 30.8 us -> none  [level_pass(): picked = jnp.take(row_store, source[0, 0, 0], axis=0)]
  transfers between devices with their start and end apart: 5 -> 43, of which waited for: 5 -> 30; matrix products, arithmetic and copies ran while one was open for 0% -> 7% of each run, Pallas kernels for 0% -> 10%
where the time goes in v1:
time: 213 us; the launch traced here: 215 us
  waiting for transfers between devices  91.7 us (43%)
  starting transfers between devices  55 us (26%)
  Pallas kernels  45.3 us (21%)
  local copies, waits for them, and re-layouts  17.9 us (8%)
  other arithmetic  3.94 us (2%)
    ppermute x30, waiting for transfers between devices, shift(): return lax.ppermute(a, 'pcol', pairs)  70.3 us
    ppermute x30, starting transfers between devices, shift(): return lax.ppermute(a, 'pcol', pairs)  49.1 us
    pallas_call x6, Pallas kernels, tile_products(): pl.pallas_call(functools.partial(products_kernel, tuple(columns), tuple(s...  31.7 us
    ppermute x13, waiting for transfers between devices, swap(): return lax.ppermute(a, axis, [(0, 1), (1, 0)])  21.5 us
    unnamed x50, local copies, waits for them, and re-layouts  8 us
    pallas_call x3, Pallas kernels, solve(): pl.pallas_call(solve_kernel, out_shape=(jax.ShapeDtypeStruct(seed.shape,...  7.28 us
    pallas_call x1, Pallas kernels, top_products(): pl.pallas_call(functools.partial(top_kernel, per_dev), out_shape=[jax.Sha...  6.25 us
    ppermute x13, starting transfers between devices, swap(): return lax.ppermute(a, axis, [(0, 1), (1, 0)])  5.99 us
  transfers between devices with their start and end apart: 43, of which 30 were waited for; matrix products, arithmetic and copies ran while one was open for 7% of the time, Pallas kernels for 10%

profile of v1, /device:TPU:10, one launch (start us, length us, event | category | flops | bytes accessed | tf_op | source)
XLA Modules:
  0.0 214.8 jit_solution(8313290956748623265)
XLA Ops:
  0.6 6.2 %shard_map.175 = (bf16[2,256,256]{2,1,0:T(8,128)(2,1)}, bf16[2,256,256]{2,1,0:T(8,128)(2,1)}) custom-call(s32[1]{0:T(128)} %bitcast.1.row, s32[58]{0:T(128)} %bitcast.48, s32[58]{0:T(128)} %bitcast.49, bf16[2,256,256]{2,1,0:T(8,128)(2,1)} %bitcast.33, bf16[58,256,256]{2,1,0:T(8,128)(2,1)} %bitcast.32), custom_call_target="tpu_custom_call" | custom-call | tf_op jit(solution)/shard_map/pallas_call | solution.py:150
  9.1 7.6 %collective-permute-done.other = bf16[2,256,256]{2,1,0:T(8,128)(2,1)S(1)} collective-permute-done((bf16[2,256,256]{2,1,0:T(8,128)(2,1)}, bf16[2,256,256]{2,1,0:T(8,128)(2,1)S(1)}, u32[]{:S(2)}, u32[]{:S(2)}) %collective-permute-start) | collective-permute-done | bytes 262176 | tf_op jit(solution)/shard_map/ppermute | solution.py:183
  17.5 2.4 %shard_map.176 = (f32[2,256,256]{2,1,0:T(8,128)}, bf16[2,256,256]{2,1,0:T(8,128)(2,1)}) custom-call(f32[2,256,256]{2,1,0:T(8,128)} %bitcast.38, bf16[2,256,256]{2,1,0:T(8,128)(2,1)} %get-tuple-element.37.mine, bf16[2,256,256]{2,1,0:T(8,128)(2,1)} %copy-done.16, bf16[2,256,256]{2,1,0:T(8,128)(2,1)} %bitcast.41), custom_call_target="tpu_custom_call" | custom-call | tf_op jit(solution)/shard_map/pallas_call | solution.py:174
  22.1 5.2 %collective-permute-done.1 = bf16[2,256,256]{2,1,0:T(8,128)(2,1)S(1)} collective-permute-done((bf16[2,256,256]{2,1,0:T(8,128)(2,1)}, bf16[2,256,256]{2,1,0:T(8,128)(2,1)S(1)}, u32[]{:S(2)}, u32[]{:S(2)}) %collective-permute-start.1) | collective-permute-done | bytes 262176 | tf_op jit(solution)/shard_map/ppermute | solution.py:195
  36.1 2.3 %collective-permute-done.5 = bf16[2,256,256]{2,1,0:T(8,128)(2,1)S(1)} collective-permute-done((bf16[2,256,256]{2,1,0:T(8,128)(2,1)S(1)}, bf16[2,256,256]{2,1,0:T(8,128)(2,1)S(1)}, u32[]{:S(2)}, u32[]{:S(2)}) %collective-permute-start.5) | collective-permute-done | bytes 262176 | tf_op jit(solution)/shard_map/ppermute | solution.py:195
  38.4 2.3 %collective-permute-start.4 = (bf16[2,256,256]{2,1,0:T(8,128)(2,1)S(1)}, bf16[2,256,256]{2,1,0:T(8,128)(2,1)S(1)}, u32[]{:S(2)}, u32[]{:S(2)}) collective-permute-start(bf16[2,256,256]{2,1,0:T(8,128)(2,1)S(1)} %pad_maximum_fusion), channel_id=1, source_target_pairs={{0,4},{1,5},{2,6},{3,7},{4,0},{5,1},{6,2},{7,3},{8,12},{9,13},{10,... | collective-permute-start | bytes 786440 | tf_op jit(solution)/shard_map/ppermute | solution.py:195
  49.9 3.8 %collective-permute-start.8 = (bf16[8,256,256]{2,1,0:T(8,128)(2,1)}, bf16[8,256,256]{2,1,0:T(8,128)(2,1)S(1)}, u32[]{:S(2)}, u32[]{:S(2)}) collective-permute-start(bf16[8,256,256]{2,1,0:T(8,128)(2,1)} %constant_dynamic-update-slice_fusion.refs_4_), channel_id=1, source_target_pairs={{0,8},{1,9},{2,10},{3,11},{4,12},{5,13},{6,14},{7,15},{8,16},{9,17... | collective-permute-start | bytes 3145736 | tf_op jit(solution)/shard_map/ppermute | solution.py:195
  53.7 15.3 %collective-permute-done.10.refs_10_ = bf16[8,256,256]{2,1,0:T(8,128)(2,1)S(1)} collective-permute-done((bf16[8,256,256]{2,1,0:T(8,128)(2,1)S(1)}, bf16[8,256,256]{2,1,0:T(8,128)(2,1)S(1)}, u32[]{:S(2)}, u32[]{:S(2)}) %collective-permute-start.10) | collective-permute-done | bytes 1048608 | tf_op jit(solution)/shard_map/ppermute | solution.py:195
  70.4 2.9 %collective-permute-done.8.refs_5_ = bf16[8,256,256]{2,1,0:T(8,128)(2,1)S(1)} collective-permute-done((bf16[8,256,256]{2,1,0:T(8,128)(2,1)}, bf16[8,256,256]{2,1,0:T(8,128)(2,1)S(1)}, u32[]{:S(2)}, u32[]{:S(2)}) %collective-permute-start.8) | collective-permute-done | bytes 1048608 | tf_op jit(solution)/shard_map/ppermute | solution.py:195
  74.4 2.7 %collective-permute-start.13 = (bf16[4,256,256]{2,1,0:T(8,128)(2,1)S(1)}, bf16[4,256,256]{2,1,0:T(8,128)(2,1)}, u32[]{:S(2)}, u32[]{:S(2)}) collective-permute-start(bf16[4,256,256]{2,1,0:T(8,128)(2,1)S(1)} %slice.53), channel_id=1, source_target_pairs={{0,24},{1,25},{2,26},{3,27},{4,28},{5,29},{6,30},{7,31},{8,0},{9,1... | collective-permute-start | bytes 1572872 | tf_op jit(solution)/shard_map/ppermute | solution.py:195
  79.4 4.5 %collective-permute-done.12.refs_7_ = bf16[4,256,256]{2,1,0:T(8,128)(2,1)} collective-permute-done((bf16[4,256,256]{2,1,0:T(8,128)(2,1)S(1)}, bf16[4,256,256]{2,1,0:T(8,128)(2,1)}, u32[]{:S(2)}, u32[]{:S(2)}) %collective-permute-start.12) | collective-permute-done | bytes 524320 | tf_op jit(solution)/shard_map/ppermute | solution.py:195
  83.9 2.5 %collective-permute-done.14.refs_12_ = bf16[4,256,256]{2,1,0:T(8,128)(2,1)} collective-permute-done((bf16[4,256,256]{2,1,0:T(8,128)(2,1)S(1)}, bf16[4,256,256]{2,1,0:T(8,128)(2,1)}, u32[]{:S(2)}, u32[]{:S(2)}) %collective-permute-start.14) | collective-permute-done | bytes 524320 | tf_op jit(solution)/shard_map/ppermute | solution.py:195
  89.8 2.6 %collective-permute-done.19.refs_17_ = bf16[4,256,256]{2,1,0:T(8,128)(2,1)} collective-permute-done((bf16[4,256,256]{2,1,0:T(8,128)(2,1)}, bf16[4,256,256]{2,1,0:T(8,128)(2,1)}, u32[]{:S(2)}, u32[]{:S(2)}) %collective-permute-start.19) | collective-permute-done | bytes 524320 | tf_op jit(solution)/shard_map/ppermute | solution.py:183
  97.9 2.6 %collective-permute-done.21.refs_19_ = bf16[8,256,256]{2,1,0:T(8,128)(2,1)S(1)} collective-permute-done((bf16[8,256,256]{2,1,0:T(8,128)(2,1)}, bf16[8,256,256]{2,1,0:T(8,128)(2,1)S(1)}, u32[]{:S(2)}, u32[]{:S(2)}) %collective-permute-start.21) | collective-permute-done | bytes 1048608 | tf_op jit(solution)/shard_map/ppermute | solution.py:183
  102.8 5.4 %shard_map.178 = bf16[2,256,256]{2,1,0:T(8,128)(2,1)} custom-call(s32[58]{0:T(128)} %get-tuple-element.74.refs_0_, s32[58]{0:T(128)} %get-tuple-element.73.refs_1_, s32[125]{0:T(128)} %convert_reduce_fusion.2.refs_2_, bf16[2,256,256]{2,1,0:T(8,128)(2,1)} %bitcast.34, bf16[8,256,256]{2,1,0:T(8,128)(2,1)} %constant_dynamic-update-slice_fusion.refs_4_, ...), custom_call_target="tpu_custom_call" | custom-call | flops 973078528 | bytes 7602176 | tf_op jit(solution)/shard_map/pallas_call | solution.py:95
  110.0 6.9 %shard_map.177.mine = bf16[2,256,256]{2,1,0:T(8,128)(2,1)} custom-call(s32[58]{0:T(128)} %get-tuple-element.74.refs_0_, s32[58]{0:T(128)} %get-tuple-element.73.refs_1_, s32[125]{0:T(128)} %convert_reduce_fusion.2.refs_2_, bf16[2,256,256]{2,1,0:T(8,128)(2,1)} %bitcast.35, bf16[8,256,256]{2,1,0:T(8,128)(2,1)} %constant_dynamic-update-slice_fusion.refs_4_, ...), custom_call_target="tpu_custom_call" | custom-call | flops 973078528 | bytes 7602176 | tf_op jit(solution)/shard_map/pallas_call | solution.py:95
  119.6 2.4 %shard_map.179 = (f32[2,256,256]{2,1,0:T(8,128)}, bf16[2,256,256]{2,1,0:T(8,128)(2,1)}) custom-call(f32[2,256,256]{2,1,0:T(8,128)} %bitcast.39, bf16[2,256,256]{2,1,0:T(8,128)(2,1)} %shard_map.177.mine, bf16[2,256,256]{2,1,0:T(8,128)(2,1)} %copy-done.15, bf16[2,256,256]{2,1,0:T(8,128)(2,1)} %bitcast.42), custom_call_target="tpu_custom_call" | custom-call | tf_op jit(solution)/shard_map/pallas_call | solution.py:174
  125.2 5.4 %collective-permute-done.27 = bf16[2,256,256]{2,1,0:T(8,128)(2,1)S(1)} collective-permute-done((bf16[2,256,256]{2,1,0:T(8,128)(2,1)}, bf16[2,256,256]{2,1,0:T(8,128)(2,1)S(1)}, u32[]{:S(2)}, u32[]{:S(2)}) %collective-permute-start.27) | collective-permute-done | bytes 262176 | tf_op jit(solution)/shard_map/ppermute | solution.py:195
  131.5 3.2 %collective-permute-start.32 = (bf16[2,256,256]{2,1,0:T(8,128)(2,1)S(1)}, bf16[2,256,256]{2,1,0:T(8,128)(2,1)S(1)}, u32[]{:S(2)}, u32[]{:S(2)}) collective-permute-start(bf16[2,256,256]{2,1,0:T(8,128)(2,1)S(1)} %pad_maximum_fusion.3), channel_id=1, source_target_pairs={{0,24},{1,25},{2,26},{3,27},{4,28},{5,29},{6,30},{7,31},{8,0},{9,1... | collective-permute-start | bytes 786440 | tf_op jit(solution)/shard_map/ppermute | solution.py:195
  138.1 3.7 %collective-permute-done.31 = bf16[2,256,256]{2,1,0:T(8,128)(2,1)S(1)} collective-permute-done((bf16[2,256,256]{2,1,0:T(8,128)(2,1)S(1)}, bf16[2,256,256]{2,1,0:T(8,128)(2,1)S(1)}, u32[]{:S(2)}, u32[]{:S(2)}) %collective-permute-start.31) | collective-permute-done | bytes 262176 | tf_op jit(solution)/shard_map/ppermute | solution.py:195
  141.8 7.8 %collective-permute-start.30 = (bf16[2,256,256]{2,1,0:T(8,128)(2,1)S(1)}, bf16[2,256,256]{2,1,0:T(8,128)(2,1)S(1)}, u32[]{:S(2)}, u32[]{:S(2)}) collective-permute-start(bf16[2,256,256]{2,1,0:T(8,128)(2,1)S(1)} %pad_maximum_fusion.2), channel_id=1, source_target_pairs={{0,4},{1,5},{2,6},{3,7},{4,0},{5,1},{6,2},{7,3},{8,12},{9,13},{10,... | collective-permute-start | bytes 786440 | tf_op jit(solution)/shard_map/ppermute | solution.py:195
  155.3 3.2 %collective-permute-start.35 = (bf16[8,256,256]{2,1,0:T(8,128)(2,1)}, bf16[8,256,256]{2,1,0:T(8,128)(2,1)S(1)}, u32[]{:S(2)}, u32[]{:S(2)}) collective-permute-start(bf16[8,256,256]{2,1,0:T(8,128)(2,1)} %constant_dynamic-update-slice_fusion.10.refs_3_), channel_id=1, source_target_pairs={{0,24},{1,25},{2,26},{3,27},{4,28},{5,29},{6,30},{7,31},{8,0},{9,1... | collective-permute-start | bytes 3145736 | tf_op jit(solution)/shard_map/ppermute | solution.py:195
  163.2 4.9 %shard_map.181.refs_14_ = f32[2,256,256]{2,1,0:T(8,128)} custom-call(s32[58]{0:T(128)} %get-tuple-element.72.refs_0_, s32[58]{0:T(128)} %get-tuple-element.71.refs_1_, s32[125]{0:T(128)} %convert_reduce_fusion.refs_2_, bf16[2,256,256]{2,1,0:T(8,128)(2,1)} %bitcast.36, bf16[8,256,256]{2,1,0:T(8,128)(2,1)} %constant_dynamic-update-slice_fusion.refs_4_, ...), custom_call_target="tpu_custom_call" | custom-call | flops 973078528 | bytes 7602176 | tf_op jit(solution)/shard_map/pallas_call | solution.py:95
  168.1 5.1 %shard_map.180.refs_14_ = f32[2,256,256]{2,1,0:T(8,128)} custom-call(s32[58]{0:T(128)} %get-tuple-element.72.refs_0_, s32[58]{0:T(128)} %get-tuple-element.71.refs_1_, s32[125]{0:T(128)} %convert_reduce_fusion.refs_2_, bf16[2,256,256]{2,1,0:T(8,128)(2,1)} %bitcast.37, bf16[8,256,256]{2,1,0:T(8,128)(2,1)} %constant_dynamic-update-slice_fusion.refs_4_, ...), custom_call_target="tpu_custom_call" | custom-call | flops 973078528 | bytes 7602176 | tf_op jit(solution)/shard_map/pallas_call | solution.py:95
  173.2 6.5 %collective-permute-done.34.refs_4_ = bf16[8,256,256]{2,1,0:T(8,128)(2,1)S(1)} collective-permute-done((bf16[8,256,256]{2,1,0:T(8,128)(2,1)}, bf16[8,256,256]{2,1,0:T(8,128)(2,1)S(1)}, u32[]{:S(2)}, u32[]{:S(2)}) %collective-permute-start.34) | collective-permute-done | bytes 1048608 | tf_op jit(solution)/shard_map/ppermute | solution.py:195
  183.0 3.3 %collective-permute-start.39 = (bf16[4,256,256]{2,1,0:T(8,128)(2,1)S(1)}, bf16[4,256,256]{2,1,0:T(8,128)(2,1)}, u32[]{:S(2)}, u32[]{:S(2)}) collective-permute-start(bf16[4,256,256]{2,1,0:T(8,128)(2,1)S(1)} %slice.61), channel_id=1, source_target_pairs={{0,24},{1,25},{2,26},{3,27},{4,28},{5,29},{6,30},{7,31},{8,0},{9,1... | collective-permute-start | bytes 1572872 | tf_op jit(solution)/shard_map/ppermute | solution.py:195
  189.7 4.3 %collective-permute-done.38.refs_6_ = bf16[4,256,256]{2,1,0:T(8,128)(2,1)S(1)} collective-permute-done((bf16[4,256,256]{2,1,0:T(8,128)(2,1)S(1)}, bf16[4,256,256]{2,1,0:T(8,128)(2,1)S(1)}, u32[]{:S(2)}, u32[]{:S(2)}) %collective-permute-start.38) | collective-permute-done | bytes 524320 | tf_op jit(solution)/shard_map/ppermute | solution.py:195
  195.9 2.9 %collective-permute-done.41.refs_12_ = bf16[4,256,256]{2,1,0:T(8,128)(2,1)} collective-permute-done((bf16[4,256,256]{2,1,0:T(8,128)(2,1)S(1)}, bf16[4,256,256]{2,1,0:T(8,128)(2,1)}, u32[]{:S(2)}, u32[]{:S(2)}) %collective-permute-start.41) | collective-permute-done | bytes 524320 | tf_op jit(solution)/shard_map/ppermute | solution.py:195
  198.7 4.8 %shard_map.183 = bf16[2,256,256]{2,1,0:T(8,128)(2,1)} custom-call(s32[58]{0:T(128)} %get-tuple-element.72.refs_0_, s32[58]{0:T(128)} %get-tuple-element.71.refs_1_, s32[125]{0:T(128)} %convert_reduce_fusion.refs_2_, bf16[8,256,256]{2,1,0:T(8,128)(2,1)} %constant_dynamic-update-slice_fusion.10.refs_3_, bf16[8,256,256]{2,1,0:T(8,128)(2,1)} %copy-done.10, ...), custom_call_target="tpu_custom_call" | custom-call | flops 973078528 | bytes 7602176 | tf_op jit(solution)/shard_map/pallas_call | solution.py:95
  203.6 4.6 %shard_map.182.mine = bf16[2,256,256]{2,1,0:T(8,128)(2,1)} custom-call(s32[58]{0:T(128)} %get-tuple-element.72.refs_0_, s32[58]{0:T(128)} %get-tuple-element.71.refs_1_, s32[125]{0:T(128)} %convert_reduce_fusion.refs_2_, bf16[8,256,256]{2,1,0:T(8,128)(2,1)} %constant_dynamic-update-slice_fusion.10.refs_3_, bf16[8,256,256]{2,1,0:T(8,128)(2,1)} %copy-done.10, ...), custom_call_target="tpu_custom_call" | custom-call | flops 973078528 | bytes 7602176 | tf_op jit(solution)/shard_map/pallas_call | solution.py:95
  208.2 3.5 %collective-permute-done.42.other = bf16[2,256,256]{2,1,0:T(8,128)(2,1)S(1)} collective-permute-done((bf16[2,256,256]{2,1,0:T(8,128)(2,1)}, bf16[2,256,256]{2,1,0:T(8,128)(2,1)S(1)}, u32[]{:S(2)}, u32[]{:S(2)}) %collective-permute-start.42) | collective-permute-done | bytes 262176 | tf_op jit(solution)/shard_map/ppermute | solution.py:183
  212.4 2.4 %shard_map.184 = (f32[2,256,256]{2,1,0:T(8,128)}, bf16[2,256,256]{2,1,0:T(8,128)(2,1)}) custom-call(f32[2,256,256]{2,1,0:T(8,128)} %bitcast.40, bf16[2,256,256]{2,1,0:T(8,128)(2,1)} %shard_map.182.mine, bf16[2,256,256]{2,1,0:T(8,128)(2,1)} %copy-done.14, bf16[2,256,256]{2,1,0:T(8,128)(2,1)} %bitcast.43), custom_call_target="tpu_custom_call" | custom-call | tf_op jit(solution)/shard_map/pallas_call | solution.py:174
  (149 shorter events, 70.4 us)
Async XLA Ops:
  6.9 9.8 %collective-permute-start = (bf16[2,256,256]{2,1,0:T(8,128)(2,1)}, bf16[2,256,256]{2,1,0:T(8,128)(2,1)S(1)}, u32[]{:S(2)}, u32[]{:S(2)}) collective-permute-start(bf16[2,256,256]{2,1,0:T(8,128)(2,1)} %get-tuple-element.38), channel_id=1, source_target_pairs={{0,32},{32,0},{1,33},{33,1},{2,34},{34,2},{3,35},{35,3},{4,36},{36... | collective-permute-start | bytes 786440 | tf_op jit(solution)/shard_map/ppermute | solution.py:183
  28.0 10.4 %collective-permute-start.5 = (bf16[2,256,256]{2,1,0:T(8,128)(2,1)S(1)}, bf16[2,256,256]{2,1,0:T(8,128)(2,1)S(1)}, u32[]{:S(2)}, u32[]{:S(2)}) collective-permute-start(bf16[2,256,256]{2,1,0:T(8,128)(2,1)S(1)} %pad_maximum_fusion.1), channel_id=1, source_target_pairs={{0,8},{1,9},{2,10},{3,11},{4,12},{5,13},{6,14},{7,15},{8,16},{9,17... | collective-permute-start | bytes 786440 | tf_op jit(solution)/shard_map/ppermute | solution.py:195
  30.0 11.6 %collective-permute-start.6 = (bf16[2,256,256]{2,1,0:T(8,128)(2,1)S(1)}, bf16[2,256,256]{2,1,0:T(8,128)(2,1)S(1)}, u32[]{:S(2)}, u32[]{:S(2)}) collective-permute-start(bf16[2,256,256]{2,1,0:T(8,128)(2,1)S(1)} %pad_maximum_fusion.1), channel_id=1, source_target_pairs={{0,24},{1,25},{2,26},{3,27},{4,28},{5,29},{6,30},{7,31},{8,0},{9,1... | collective-permute-start | bytes 786440 | tf_op jit(solution)/shard_map/ppermute | solution.py:195
  32.2 11.2 %collective-permute-start.7 = (bf16[2,256,256]{2,1,0:T(8,128)(2,1)S(1)}, bf16[2,256,256]{2,1,0:T(8,128)(2,1)S(1)}, u32[]{:S(2)}, u32[]{:S(2)}) collective-permute-start(bf16[2,256,256]{2,1,0:T(8,128)(2,1)S(1)} %pad_maximum_fusion.1), channel_id=1, source_target_pairs={{0,16},{1,17},{2,18},{3,19},{4,20},{5,21},{6,22},{7,23},{8,24},{9,... | collective-permute-start | bytes 786440 | tf_op jit(solution)/shard_map/ppermute | solution.py:195
  34.0 9.4 %collective-permute-start.2 = (bf16[2,256,256]{2,1,0:T(8,128)(2,1)S(1)}, bf16[2,256,256]{2,1,0:T(8,128)(2,1)S(1)}, u32[]{:S(2)}, u32[]{:S(2)}) collective-permute-start(bf16[2,256,256]{2,1,0:T(8,128)(2,1)S(1)} %pad_maximum_fusion), channel_id=1, source_target_pairs={{0,2},{1,3},{2,4},{3,5},{4,6},{5,7},{6,0},{7,1},{8,10},{9,11},{10,... | collective-permute-start | bytes 786440 | tf_op jit(solution)/shard_map/ppermute | solution.py:195
  35.7 8.7 %collective-permute-start.3 = (bf16[2,256,256]{2,1,0:T(8,128)(2,1)S(1)}, bf16[2,256,256]{2,1,0:T(8,128)(2,1)S(1)}, u32[]{:S(2)}, u32[]{:S(2)}) collective-permute-start(bf16[2,256,256]{2,1,0:T(8,128)(2,1)S(1)} %pad_maximum_fusion), channel_id=1, source_target_pairs={{0,6},{1,7},{2,0},{3,1},{4,2},{5,3},{6,4},{7,5},{8,14},{9,15},{10,... | collective-permute-start | bytes 786440 | tf_op jit(solution)/shard_map/ppermute | solution.py:195
  38.4 8.7 %collective-permute-start.4 = (bf16[2,256,256]{2,1,0:T(8,128)(2,1)S(1)}, bf16[2,256,256]{2,1,0:T(8,128)(2,1)S(1)}, u32[]{:S(2)}, u32[]{:S(2)}) collective-permute-start(bf16[2,256,256]{2,1,0:T(8,128)(2,1)S(1)} %pad_maximum_fusion), channel_id=1, source_target_pairs={{0,4},{1,5},{2,6},{3,7},{4,0},{5,1},{6,2},{7,3},{8,12},{9,13},{10,... | collective-permute-start | bytes 786440 | tf_op jit(solution)/shard_map/ppermute | solution.py:195
  47.9 21.1 %collective-permute-start.10 = (bf16[8,256,256]{2,1,0:T(8,128)(2,1)S(1)}, bf16[8,256,256]{2,1,0:T(8,128)(2,1)S(1)}, u32[]{:S(2)}, u32[]{:S(2)}) collective-permute-start(bf16[8,256,256]{2,1,0:T(8,128)(2,1)S(1)} %constant_dynamic-update-slice_fusion.5.refs_9_), channel_id=1, source_target_pairs={{0,2},{1,3},{2,4},{3,5},{4,6},{5,7},{6,0},{7,1},{8,10},{9,11},{10,... | collective-permute-start | bytes 3145736 | tf_op jit(solution)/shard_map/ppermute | solution.py:195
  48.6 21.7 %collective-permute-start.11 = (bf16[8,256,256]{2,1,0:T(8,128)(2,1)S(1)}, bf16[8,256,256]{2,1,0:T(8,128)(2,1)S(1)}, u32[]{:S(2)}, u32[]{:S(2)}) collective-permute-start(bf16[8,256,256]{2,1,0:T(8,128)(2,1)S(1)} %constant_dynamic-update-slice_fusion.5.refs_9_), channel_id=1, source_target_pairs={{0,6},{1,7},{2,0},{3,1},{4,2},{5,3},{6,4},{7,5},{8,14},{9,15},{10,... | collective-permute-start | bytes 3145736 | tf_op jit(solution)/shard_map/ppermute | solution.py:195
  49.9 23.4 %collective-permute-start.8 = (bf16[8,256,256]{2,1,0:T(8,128)(2,1)}, bf16[8,256,256]{2,1,0:T(8,128)(2,1)S(1)}, u32[]{:S(2)}, u32[]{:S(2)}) collective-permute-start(bf16[8,256,256]{2,1,0:T(8,128)(2,1)} %constant_dynamic-update-slice_fusion.refs_4_), channel_id=1, source_target_pairs={{0,8},{1,9},{2,10},{3,11},{4,12},{5,13},{6,14},{7,15},{8,16},{9,17... | collective-permute-start | bytes 3145736 | tf_op jit(solution)/shard_map/ppermute | solution.py:195
  53.6 19.7 %collective-permute-start.9 = (bf16[8,256,256]{2,1,0:T(8,128)(2,1)}, bf16[8,256,256]{2,1,0:T(8,128)(2,1)S(1)}, u32[]{:S(2)}, u32[]{:S(2)}) collective-permute-start(bf16[8,256,256]{2,1,0:T(8,128)(2,1)} %constant_dynamic-update-slice_fusion.refs_4_), channel_id=1, source_target_pairs={{0,24},{1,25},{2,26},{3,27},{4,28},{5,29},{6,30},{7,31},{8,0},{9,1... | collective-permute-start | bytes 3145736 | tf_op jit(solution)/shard_map/ppermute | solution.py:195
  73.3 10.6 %collective-permute-start.12 = (bf16[4,256,256]{2,1,0:T(8,128)(2,1)S(1)}, bf16[4,256,256]{2,1,0:T(8,128)(2,1)}, u32[]{:S(2)}, u32[]{:S(2)}) collective-permute-start(bf16[4,256,256]{2,1,0:T(8,128)(2,1)S(1)} %slice.52), channel_id=1, source_target_pairs={{0,8},{1,9},{2,10},{3,11},{4,12},{5,13},{6,14},{7,15},{8,16},{9,17... | collective-permute-start | bytes 1572872 | tf_op jit(solution)/shard_map/ppermute | solution.py:195
  74.4 9.6 %collective-permute-start.13 = (bf16[4,256,256]{2,1,0:T(8,128)(2,1)S(1)}, bf16[4,256,256]{2,1,0:T(8,128)(2,1)}, u32[]{:S(2)}, u32[]{:S(2)}) collective-permute-start(bf16[4,256,256]{2,1,0:T(8,128)(2,1)S(1)} %slice.53), channel_id=1, source_target_pairs={{0,24},{1,25},{2,26},{3,27},{4,28},{5,29},{6,30},{7,31},{8,0},{9,1... | collective-permute-start | bytes 1572872 | tf_op jit(solution)/shard_map/ppermute | solution.py:195
  77.1 9.4 %collective-permute-start.14 = (bf16[4,256,256]{2,1,0:T(8,128)(2,1)S(1)}, bf16[4,256,256]{2,1,0:T(8,128)(2,1)}, u32[]{:S(2)}, u32[]{:S(2)}) collective-permute-start(bf16[4,256,256]{2,1,0:T(8,128)(2,1)S(1)} %slice.54), channel_id=1, source_target_pairs={{0,2},{1,3},{2,4},{3,5},{4,6},{5,7},{6,0},{7,1},{8,10},{9,11},{10,... | collective-permute-start | bytes 1572872 | tf_op jit(solution)/shard_map/ppermute | solution.py:195
  79.3 9.4 %collective-permute-start.15 = (bf16[4,256,256]{2,1,0:T(8,128)(2,1)S(1)}, bf16[4,256,256]{2,1,0:T(8,128)(2,1)}, u32[]{:S(2)}, u32[]{:S(2)}) collective-permute-start(bf16[4,256,256]{2,1,0:T(8,128)(2,1)S(1)} %slice.55), channel_id=1, source_target_pairs={{0,6},{1,7},{2,0},{3,1},{4,2},{5,3},{6,4},{7,5},{8,14},{9,15},{10,... | collective-permute-start | bytes 1572872 | tf_op jit(solution)/shard_map/ppermute | solution.py:195
  108.2 10.7 %collective-permute-start.26 = (bf16[2,256,256]{2,1,0:T(8,128)(2,1)}, bf16[2,256,256]{2,1,0:T(8,128)(2,1)S(1)}, u32[]{:S(2)}, u32[]{:S(2)}) collective-permute-start(bf16[2,256,256]{2,1,0:T(8,128)(2,1)} %shard_map.178), channel_id=1, source_target_pairs={{0,32},{32,0},{1,33},{33,1},{2,34},{34,2},{3,35},{35,3},{4,36},{36... | collective-permute-start | bytes 786440 | tf_op jit(solution)/shard_map/ppermute | solution.py:183
  122.1 8.5 %collective-permute-start.27 = (bf16[2,256,256]{2,1,0:T(8,128)(2,1)}, bf16[2,256,256]{2,1,0:T(8,128)(2,1)S(1)}, u32[]{:S(2)}, u32[]{:S(2)}) collective-permute-start(bf16[2,256,256]{2,1,0:T(8,128)(2,1)} %get-tuple-element.61), channel_id=1, source_target_pairs={{0,1},{1,0},{2,3},{3,2},{4,5},{5,4},{6,7},{7,6},{8,9},{9,8},{10,11... | collective-permute-start | bytes 786440 | tf_op jit(solution)/shard_map/ppermute | solution.py:195
  131.4 10.4 %collective-permute-start.31 = (bf16[2,256,256]{2,1,0:T(8,128)(2,1)S(1)}, bf16[2,256,256]{2,1,0:T(8,128)(2,1)S(1)}, u32[]{:S(2)}, u32[]{:S(2)}) collective-permute-start(bf16[2,256,256]{2,1,0:T(8,128)(2,1)S(1)} %pad_maximum_fusion.3), channel_id=1, source_target_pairs={{0,8},{1,9},{2,10},{3,11},{4,12},{5,13},{6,14},{7,15},{8,16},{9,17... | collective-permute-start | bytes 786440 | tf_op jit(solution)/shard_map/ppermute | solution.py:195
  131.5 18.8 %collective-permute-start.32 = (bf16[2,256,256]{2,1,0:T(8,128)(2,1)S(1)}, bf16[2,256,256]{2,1,0:T(8,128)(2,1)S(1)}, u32[]{:S(2)}, u32[]{:S(2)}) collective-permute-start(bf16[2,256,256]{2,1,0:T(8,128)(2,1)S(1)} %pad_maximum_fusion.3), channel_id=1, source_target_pairs={{0,24},{1,25},{2,26},{3,27},{4,28},{5,29},{6,30},{7,31},{8,0},{9,1... | collective-permute-start | bytes 786440 | tf_op jit(solution)/shard_map/ppermute | solution.py:195
  134.7 16.4 %collective-permute-start.33 = (bf16[2,256,256]{2,1,0:T(8,128)(2,1)S(1)}, bf16[2,256,256]{2,1,0:T(8,128)(2,1)S(1)}, u32[]{:S(2)}, u32[]{:S(2)}) collective-permute-start(bf16[2,256,256]{2,1,0:T(8,128)(2,1)S(1)} %pad_maximum_fusion.3), channel_id=1, source_target_pairs={{0,16},{1,17},{2,18},{3,19},{4,20},{5,21},{6,22},{7,23},{8,24},{9,... | collective-permute-start | bytes 786440 | tf_op jit(solution)/shard_map/ppermute | solution.py:195
  134.8 16.9 %collective-permute-start.28 = (bf16[2,256,256]{2,1,0:T(8,128)(2,1)S(1)}, bf16[2,256,256]{2,1,0:T(8,128)(2,1)S(1)}, u32[]{:S(2)}, u32[]{:S(2)}) collective-permute-start(bf16[2,256,256]{2,1,0:T(8,128)(2,1)S(1)} %pad_maximum_fusion.2), channel_id=1, source_target_pairs={{0,2},{1,3},{2,4},{3,5},{4,6},{5,7},{6,0},{7,1},{8,10},{9,11},{10,... | collective-permute-start | bytes 786440 | tf_op jit(solution)/shard_map/ppermute | solution.py:195
  135.8 16.7 %collective-permute-start.29 = (bf16[2,256,256]{2,1,0:T(8,128)(2,1)S(1)}, bf16[2,256,256]{2,1,0:T(8,128)(2,1)S(1)}, u32[]{:S(2)}, u32[]{:S(2)}) collective-permute-start(bf16[2,256,256]{2,1,0:T(8,128)(2,1)S(1)} %pad_maximum_fusion.2), channel_id=1, source_target_pairs={{0,6},{1,7},{2,0},{3,1},{4,2},{5,3},{6,4},{7,5},{8,14},{9,15},{10,... | collective-permute-start | bytes 786440 | tf_op jit(solution)/shard_map/ppermute | solution.py:195
  141.8 12.8 %collective-permute-start.30 = (bf16[2,256,256]{2,1,0:T(8,128)(2,1)S(1)}, bf16[2,256,256]{2,1,0:T(8,128)(2,1)S(1)}, u32[]{:S(2)}, u32[]{:S(2)}) collective-permute-start(bf16[2,256,256]{2,1,0:T(8,128)(2,1)S(1)} %pad_maximum_fusion.2), channel_id=1, source_target_pairs={{0,4},{1,5},{2,6},{3,7},{4,0},{5,1},{6,2},{7,3},{8,12},{9,13},{10,... | collective-permute-start | bytes 786440 | tf_op jit(solution)/shard_map/ppermute | solution.py:195
  155.3 24.4 %collective-permute-start.34 = (bf16[8,256,256]{2,1,0:T(8,128)(2,1)}, bf16[8,256,256]{2,1,0:T(8,128)(2,1)S(1)}, u32[]{:S(2)}, u32[]{:S(2)}) collective-permute-start(bf16[8,256,256]{2,1,0:T(8,128)(2,1)} %constant_dynamic-update-slice_fusion.10.refs_3_), channel_id=1, source_target_pairs={{0,8},{1,9},{2,10},{3,11},{4,12},{5,13},{6,14},{7,15},{8,16},{9,17... | collective-permute-start | bytes 3145736 | tf_op jit(solution)/shard_map/ppermute | solution.py:195
  155.3 24.4 %collective-permute-start.35 = (bf16[8,256,256]{2,1,0:T(8,128)(2,1)}, bf16[8,256,256]{2,1,0:T(8,128)(2,1)S(1)}, u32[]{:S(2)}, u32[]{:S(2)}) collective-permute-start(bf16[8,256,256]{2,1,0:T(8,128)(2,1)} %constant_dynamic-update-slice_fusion.10.refs_3_), channel_id=1, source_target_pairs={{0,24},{1,25},{2,26},{3,27},{4,28},{5,29},{6,30},{7,31},{8,0},{9,1... | collective-permute-start | bytes 3145736 | tf_op jit(solution)/shard_map/ppermute | solution.py:195
  158.5 22.6 %collective-permute-start.36 = (bf16[8,256,256]{2,1,0:T(8,128)(2,1)}, bf16[8,256,256]{2,1,0:T(8,128)(2,1)S(1)}, u32[]{:S(2)}, u32[]{:S(2)}) collective-permute-start(bf16[8,256,256]{2,1,0:T(8,128)(2,1)} %constant_dynamic-update-slice_fusion.15.refs_8_), channel_id=1, source_target_pairs={{0,2},{1,3},{2,4},{3,5},{4,6},{5,7},{6,0},{7,1},{8,10},{9,11},{10,... | collective-permute-start | bytes 3145736 | tf_op jit(solution)/shard_map/ppermute | solution.py:195
  158.5 24.3 %collective-permute-start.37 = (bf16[8,256,256]{2,1,0:T(8,128)(2,1)}, bf16[8,256,256]{2,1,0:T(8,128)(2,1)}, u32[]{:S(2)}, u32[]{:S(2)}) collective-permute-start(bf16[8,256,256]{2,1,0:T(8,128)(2,1)} %constant_dynamic-update-slice_fusion.15.refs_8_), channel_id=1, source_target_pairs={{0,6},{1,7},{2,0},{3,1},{4,2},{5,3},{6,4},{7,5},{8,14},{9,15},{10,... | collective-permute-start | bytes 3145736 | tf_op jit(solution)/shard_map/ppermute | solution.py:195
  182.8 11.2 %collective-permute-start.38 = (bf16[4,256,256]{2,1,0:T(8,128)(2,1)S(1)}, bf16[4,256,256]{2,1,0:T(8,128)(2,1)S(1)}, u32[]{:S(2)}, u32[]{:S(2)}) collective-permute-start(bf16[4,256,256]{2,1,0:T(8,128)(2,1)S(1)} %slice.60), channel_id=1, source_target_pairs={{0,8},{1,9},{2,10},{3,11},{4,12},{5,13},{6,14},{7,15},{8,16},{9,17... | collective-permute-start | bytes 1572872 | tf_op jit(solution)/shard_map/ppermute | solution.py:195
  183.0 11.1 %collective-permute-start.39 = (bf16[4,256,256]{2,1,0:T(8,128)(2,1)S(1)}, bf16[4,256,256]{2,1,0:T(8,128)(2,1)}, u32[]{:S(2)}, u32[]{:S(2)}) collective-permute-start(bf16[4,256,256]{2,1,0:T(8,128)(2,1)S(1)} %slice.61), channel_id=1, source_target_pairs={{0,24},{1,25},{2,26},{3,27},{4,28},{5,29},{6,30},{7,31},{8,0},{9,1... | collective-permute-start | bytes 1572872 | tf_op jit(solution)/shard_map/ppermute | solution.py:195
  186.3 9.6 %collective-permute-start.40 = (bf16[4,256,256]{2,1,0:T(8,128)(2,1)S(1)}, bf16[4,256,256]{2,1,0:T(8,128)(2,1)}, u32[]{:S(2)}, u32[]{:S(2)}) collective-permute-start(bf16[4,256,256]{2,1,0:T(8,128)(2,1)S(1)} %slice.62), channel_id=1, source_target_pairs={{0,2},{1,3},{2,4},{3,5},{4,6},{5,7},{6,0},{7,1},{8,10},{9,11},{10,... | collective-permute-start | bytes 1572872 | tf_op jit(solution)/shard_map/ppermute | solution.py:195
  189.1 9.6 %collective-permute-start.41 = (bf16[4,256,256]{2,1,0:T(8,128)(2,1)S(1)}, bf16[4,256,256]{2,1,0:T(8,128)(2,1)}, u32[]{:S(2)}, u32[]{:S(2)}) collective-permute-start(bf16[4,256,256]{2,1,0:T(8,128)(2,1)S(1)} %slice.63), channel_id=1, source_target_pairs={{0,6},{1,7},{2,0},{3,1},{4,2},{5,3},{6,4},{7,5},{8,14},{9,15},{10,... | collective-permute-start | bytes 1572872 | tf_op jit(solution)/shard_map/ppermute | solution.py:195
  203.5 8.2 %collective-permute-start.42 = (bf16[2,256,256]{2,1,0:T(8,128)(2,1)}, bf16[2,256,256]{2,1,0:T(8,128)(2,1)S(1)}, u32[]{:S(2)}, u32[]{:S(2)}) collective-permute-start(bf16[2,256,256]{2,1,0:T(8,128)(2,1)} %shard_map.183), channel_id=1, source_target_pairs={{0,32},{32,0},{1,33},{33,1},{2,34},{34,2},{3,35},{35,3},{4,36},{36... | collective-permute-start | bytes 786440 | tf_op jit(solution)/shard_map/ppermute | solution.py:183
  (32 other events, 593.5 us)

commit v2 on v1

--- a/solution.py
+++ b/solution.py
@@ -110,55 +110,60 @@
     )(*operands)
 
 
-def top_kernel(per_dev, row, source, target, known, tiles, away, mine, tile_buf, total, tile_sem):
+def top_kernel(side, source, target, known, tiles, out, tile_buf, total, tile_sem):
     count = tiles.shape[0]
-    upper, depth = known.shape[0], known.shape[2]
+    upper, per_dev = known.shape[0], out.shape[0]
+    first = side[0] * per_dev
 
     def tile_copy(i):
         return pltpu.make_async_copy(tiles.at[i], tile_buf.at[i], tile_sem.at[i])
 
-    for i in range(count):
-        tile_copy(i).start()
+    def here(i):
+        return (target[i] >= first) & (target[i] < first + per_dev)
+
+    def fetch(i, carry):
+        pl.when(here(i))(lambda: tile_copy(i).start())
+        return carry
+
+    def add(i, carry):
+        @pl.when(here(i))
+        def _():
+            tile_copy(i).wait()
+            total[(target[i] - first) * upper + source[i]] += tile_buf[i].astype(F32)
+
+        return carry
+
+    lax.fori_loop(0, count, fetch, 0)
     total[...] = jnp.zeros_like(total)
-
-    def add(i, carry):
-        tile_copy(i).wait()
-        total[target[i] * upper + source[i]] += tile_buf[i].astype(F32)
-        return carry
-
     lax.fori_loop(0, count, add, 0)
-    here = row[0]
     for d in range(per_dev):
-        for out, side in ((away, 1 - here), (mine, here)):
-            first = (side * per_dev + d) * upper
-            sums = jnp.zeros(out.shape[1:], F32)
-            for k in range(upper):
-                whole = total[first + k]
-                high = whole.astype(BF16)
-                low = (whole - high.astype(F32)).astype(BF16)
-                sums += jnp.dot(known[k], high, preferred_element_type=F32)
-                sums += jnp.dot(known[k], low, preferred_element_type=F32)
-            out[d] = sums.astype(BF16)
-
-
-def top_products(source, target, known, tiles, per_dev):
+        sums = jnp.zeros(out.shape[1:], F32)
+        for k in range(upper):
+            whole = total[d * upper + k]
+            high = whole.astype(BF16)
+            low = (whole - high.astype(F32)).astype(BF16)
+            sums += jnp.dot(known[k], high, preferred_element_type=F32)
+            sums += jnp.dot(known[k], low, preferred_element_type=F32)
+        out[d] = sums.astype(BF16)
+
+
+def top_products(side, source, target, known, tiles, per_dev):
     count, depth, width = tiles.shape
     rows = known.shape[1]
     in_vmem = pl.BlockSpec(memory_space=pltpu.VMEM)
     in_smem = pl.BlockSpec(memory_space=pltpu.SMEM)
-    row = lax.axis_index("prow").astype(jnp.int32)[None]
     return pl.pallas_call(
-        functools.partial(top_kernel, per_dev),
-        out_shape=[jax.ShapeDtypeStruct((per_dev, rows, width), BF16)] * 2,
+        top_kernel,
+        out_shape=jax.ShapeDtypeStruct((per_dev, rows, width), BF16),
         in_specs=[in_smem] * 3 + [in_vmem, pl.BlockSpec(memory_space=pl.ANY)],
-        out_specs=[in_vmem] * 2,
+        out_specs=in_vmem,
         scratch_shapes=[
             pltpu.VMEM((count, depth, width), BF16),
-            pltpu.VMEM((2 * per_dev * known.shape[0], depth, width), F32),
+            pltpu.VMEM((per_dev * known.shape[0], depth, width), F32),
             pltpu.SemaphoreType.DMA((count,)),
         ],
         compiler_params=pltpu.CompilerParams(vmem_limit_bytes=60 * 1024 * 1024),
-    )(row, source, target, known, tiles)
+    )(side.astype(jnp.int32)[None], source, target, known, tiles)
 
 
 def solve_kernel(seed, mine, other, inverse, solved, rounded):
@@ -289,7 +294,8 @@
         mine = tile_products(index, mine_keys, groups, stores, tiles, dtype, init[1])
         return away, mine
 
-    away, mine = top_products(top_source, top_target, known, tiles_top, per_dev)
+    row = lax.axis_index("prow")
+    away, mine = (top_products(side, top_source, top_target, known, tiles_top, per_dev) for side in (1 - row, row))
     solved_top, rounded_top = solve(seed_top, mine, swap(away, "prow"), inverse_top)
     rounded_top, mid_source, low_source = lax.optimization_barrier((rounded_top, mid_source, low_source))
     pieces, _ = gather(rounded_top)

time: 213 us -> 211 us (level); the launches traced: 215 us -> 208 us
  starting transfers between devices: 55 us -> 48.2 us
  waiting for transfers between devices: 91.7 us -> 87.5 us
  Pallas kernels: 45.3 us -> 49.4 us
    ppermute x30, starting transfers between devices: 49.1 us -> 40 us  [shift(): return lax.ppermute(a, 'pcol', pairs)]
    ppermute x13, waiting for transfers between devices: 21.5 us -> 14.8 us  [swap(): return lax.ppermute(a, axis, [(0, 1), (1, 0)])]
    pallas_call x1 -> x2, Pallas kernels: 6.25 us -> 10.3 us  [top_products(): pl.pallas_call(top_kernel, out_shape=jax.ShapeDtypeStruct((per_dev, rows,...]
    ppermute x30, waiting for transfers between devices: 70.3 us -> 72.7 us  [shift(): return lax.ppermute(a, 'pcol', pairs)]
    ppermute x13, starting transfers between devices: 5.99 us -> 8.21 us  [swap(): return lax.ppermute(a, axis, [(0, 1), (1, 0)])]
  transfers between devices with their start and end apart: 43 -> 43, of which waited for: 30 -> 29; matrix products, arithmetic and copies ran while one was open for 7% -> 7% of each run, Pallas kernels for 10% -> 13%
where the time goes in v2:
time: 211 us; the launch traced here: 208 us
  waiting for transfers between devices  87.5 us (41%)
  Pallas kernels  49.4 us (23%)
  starting transfers between devices  48.2 us (23%)
  local copies, waits for them, and re-layouts  18.3 us (9%)
  other arithmetic  3.99 us (2%)
    ppermute x30, waiting for transfers between devices, shift(): return lax.ppermute(a, 'pcol', pairs)  72.7 us
    ppermute x30, starting transfers between devices, shift(): return lax.ppermute(a, 'pcol', pairs)  40 us
    pallas_call x6, Pallas kernels, tile_products(): pl.pallas_call(functools.partial(products_kernel, tuple(columns), tuple(s...  31.8 us
    ppermute x13, waiting for transfers between devices, swap(): return lax.ppermute(a, axis, [(0, 1), (1, 0)])  14.8 us
    pallas_call x2, Pallas kernels, top_products(): pl.pallas_call(top_kernel, out_shape=jax.ShapeDtypeStruct((per_dev, rows,...  10.3 us
    unnamed x50, local copies, waits for them, and re-layouts  8.49 us
    ppermute x13, starting transfers between devices, swap(): return lax.ppermute(a, axis, [(0, 1), (1, 0)])  8.21 us
    pallas_call x3, Pallas kernels, solve(): pl.pallas_call(solve_kernel, out_shape=(jax.ShapeDtypeStruct(seed.shape,...  7.25 us
  transfers between devices with their start and end apart: 43, of which 29 were waited for; matrix products, arithmetic and copies ran while one was open for 7% of the time, Pallas kernels for 13%

profile of v2, /device:TPU:10, one launch (start us, length us, event | category | flops | bytes accessed | tf_op | source)
XLA Modules:
  0.0 208.3 jit_solution(7366142590654500514)
XLA Ops:
  0.6 5.4 %shard_map.176 = bf16[2,256,256]{2,1,0:T(8,128)(2,1)} custom-call(s32[1]{0:T(128)} %bitcast.6.side, s32[58]{0:T(128)} %bitcast.47, s32[58]{0:T(128)} %bitcast.49, bf16[2,256,256]{2,1,0:T(8,128)(2,1)} %bitcast.35, bf16[58,256,256]{2,1,0:T(8,128)(2,1)} %bitcast.33), custom_call_target="tpu_custom_call" | custom-call | tf_op jit(solution)/shard_map/pallas_call | solution.py:155
  8.0 5.0 %shard_map.175.mine = bf16[2,256,256]{2,1,0:T(8,128)(2,1)} custom-call(s32[1]{0:T(128)} %bitcast.1.side, s32[58]{0:T(128)} %bitcast.48, s32[58]{0:T(128)} %bitcast.50, bf16[2,256,256]{2,1,0:T(8,128)(2,1)} %bitcast.36, bf16[58,256,256]{2,1,0:T(8,128)(2,1)} %bitcast.34), custom_call_target="tpu_custom_call" | custom-call | tf_op jit(solution)/shard_map/pallas_call | solution.py:155
  13.1 2.5 %collective-permute-done.other = bf16[2,256,256]{2,1,0:T(8,128)(2,1)S(1)} collective-permute-done((bf16[2,256,256]{2,1,0:T(8,128)(2,1)}, bf16[2,256,256]{2,1,0:T(8,128)(2,1)S(1)}, u32[]{:S(2)}, u32[]{:S(2)}) %collective-permute-start) | collective-permute-done | bytes 262176 | tf_op jit(solution)/shard_map/ppermute | solution.py:188
  21.0 4.6 %collective-permute-done.1 = bf16[2,256,256]{2,1,0:T(8,128)(2,1)S(1)} collective-permute-done((bf16[2,256,256]{2,1,0:T(8,128)(2,1)}, bf16[2,256,256]{2,1,0:T(8,128)(2,1)S(1)}, u32[]{:S(2)}, u32[]{:S(2)}) %collective-permute-start.1) | collective-permute-done | bytes 262176 | tf_op jit(solution)/shard_map/ppermute | solution.py:200
  28.7 2.8 %collective-permute-start.6 = (bf16[2,256,256]{2,1,0:T(8,128)(2,1)S(1)}, bf16[2,256,256]{2,1,0:T(8,128)(2,1)S(1)}, u32[]{:S(2)}, u32[]{:S(2)}) collective-permute-start(bf16[2,256,256]{2,1,0:T(8,128)(2,1)S(1)} %pad_maximum_fusion.1), channel_id=1, source_target_pairs={{0,24},{1,25},{2,26},{3,27},{4,28},{5,29},{6,30},{7,31},{8,0},{9,1... | collective-permute-start | bytes 786440 | tf_op jit(solution)/shard_map/ppermute | solution.py:200
  35.0 2.7 %collective-permute-done.5 = bf16[2,256,256]{2,1,0:T(8,128)(2,1)S(1)} collective-permute-done((bf16[2,256,256]{2,1,0:T(8,128)(2,1)S(1)}, bf16[2,256,256]{2,1,0:T(8,128)(2,1)S(1)}, u32[]{:S(2)}, u32[]{:S(2)}) %collective-permute-start.5) | collective-permute-done | bytes 262176 | tf_op jit(solution)/shard_map/ppermute | solution.py:200
  49.1 3.5 %collective-permute-start.8 = (bf16[8,256,256]{2,1,0:T(8,128)(2,1)}, bf16[8,256,256]{2,1,0:T(8,128)(2,1)S(1)}, u32[]{:S(2)}, u32[]{:S(2)}) collective-permute-start(bf16[8,256,256]{2,1,0:T(8,128)(2,1)} %constant_dynamic-update-slice_fusion.refs_4_), channel_id=1, source_target_pairs={{0,8},{1,9},{2,10},{3,11},{4,12},{5,13},{6,14},{7,15},{8,16},{9,17... | collective-permute-start | bytes 3145736 | tf_op jit(solution)/shard_map/ppermute | solution.py:200
  52.6 16.0 %collective-permute-done.10.refs_10_ = bf16[8,256,256]{2,1,0:T(8,128)(2,1)S(1)} collective-permute-done((bf16[8,256,256]{2,1,0:T(8,128)(2,1)S(1)}, bf16[8,256,256]{2,1,0:T(8,128)(2,1)S(1)}, u32[]{:S(2)}, u32[]{:S(2)}) %collective-permute-start.10) | collective-permute-done | bytes 1048608 | tf_op jit(solution)/shard_map/ppermute | solution.py:200
  69.2 3.3 %collective-permute-done.8.refs_5_ = bf16[8,256,256]{2,1,0:T(8,128)(2,1)S(1)} collective-permute-done((bf16[8,256,256]{2,1,0:T(8,128)(2,1)}, bf16[8,256,256]{2,1,0:T(8,128)(2,1)S(1)}, u32[]{:S(2)}, u32[]{:S(2)}) %collective-permute-start.8) | collective-permute-done | bytes 1048608 | tf_op jit(solution)/shard_map/ppermute | solution.py:200
  73.7 2.5 %collective-permute-start.13 = (bf16[4,256,256]{2,1,0:T(8,128)(2,1)S(1)}, bf16[4,256,256]{2,1,0:T(8,128)(2,1)}, u32[]{:S(2)}, u32[]{:S(2)}) collective-permute-start(bf16[4,256,256]{2,1,0:T(8,128)(2,1)S(1)} %slice.53), channel_id=1, source_target_pairs={{0,24},{1,25},{2,26},{3,27},{4,28},{5,29},{6,30},{7,31},{8,0},{9,1... | collective-permute-start | bytes 1572872 | tf_op jit(solution)/shard_map/ppermute | solution.py:200
  78.4 4.8 %collective-permute-done.12.refs_7_ = bf16[4,256,256]{2,1,0:T(8,128)(2,1)} collective-permute-done((bf16[4,256,256]{2,1,0:T(8,128)(2,1)S(1)}, bf16[4,256,256]{2,1,0:T(8,128)(2,1)}, u32[]{:S(2)}, u32[]{:S(2)}) %collective-permute-start.12) | collective-permute-done | bytes 524320 | tf_op jit(solution)/shard_map/ppermute | solution.py:200
  88.1 2.6 %collective-permute-done.19.refs_17_ = bf16[4,256,256]{2,1,0:T(8,128)(2,1)} collective-permute-done((bf16[4,256,256]{2,1,0:T(8,128)(2,1)}, bf16[4,256,256]{2,1,0:T(8,128)(2,1)}, u32[]{:S(2)}, u32[]{:S(2)}) %collective-permute-start.19) | collective-permute-done | bytes 524320 | tf_op jit(solution)/shard_map/ppermute | solution.py:188
  96.3 2.6 %collective-permute-done.21.refs_19_ = bf16[8,256,256]{2,1,0:T(8,128)(2,1)S(1)} collective-permute-done((bf16[8,256,256]{2,1,0:T(8,128)(2,1)}, bf16[8,256,256]{2,1,0:T(8,128)(2,1)S(1)}, u32[]{:S(2)}, u32[]{:S(2)}) %collective-permute-start.21) | collective-permute-done | bytes 1048608 | tf_op jit(solution)/shard_map/ppermute | solution.py:188
  101.2 6.2 %shard_map.179 = bf16[2,256,256]{2,1,0:T(8,128)(2,1)} custom-call(s32[58]{0:T(128)} %get-tuple-element.70.refs_0_, s32[58]{0:T(128)} %get-tuple-element.69.refs_1_, s32[125]{0:T(128)} %convert_reduce_fusion.2.refs_2_, bf16[2,256,256]{2,1,0:T(8,128)(2,1)} %bitcast.37, bf16[8,256,256]{2,1,0:T(8,128)(2,1)} %constant_dynamic-update-slice_fusion.refs_4_, ...), custom_call_target="tpu_custom_call" | custom-call | flops 973078528 | bytes 7602176 | tf_op jit(solution)/shard_map/pallas_call | solution.py:95
  109.4 6.2 %shard_map.178.mine = bf16[2,256,256]{2,1,0:T(8,128)(2,1)} custom-call(s32[58]{0:T(128)} %get-tuple-element.70.refs_0_, s32[58]{0:T(128)} %get-tuple-element.69.refs_1_, s32[125]{0:T(128)} %convert_reduce_fusion.2.refs_2_, bf16[2,256,256]{2,1,0:T(8,128)(2,1)} %bitcast.38, bf16[8,256,256]{2,1,0:T(8,128)(2,1)} %constant_dynamic-update-slice_fusion.refs_4_, ...), custom_call_target="tpu_custom_call" | custom-call | flops 973078528 | bytes 7602176 | tf_op jit(solution)/shard_map/pallas_call | solution.py:95
  118.6 2.4 %shard_map.180 = (f32[2,256,256]{2,1,0:T(8,128)}, bf16[2,256,256]{2,1,0:T(8,128)(2,1)}) custom-call(f32[2,256,256]{2,1,0:T(8,128)} %bitcast.42, bf16[2,256,256]{2,1,0:T(8,128)(2,1)} %shard_map.178.mine, bf16[2,256,256]{2,1,0:T(8,128)(2,1)} %copy-done.15, bf16[2,256,256]{2,1,0:T(8,128)(2,1)} %bitcast.45), custom_call_target="tpu_custom_call" | custom-call | tf_op jit(solution)/shard_map/pallas_call | solution.py:179
  122.7 6.4 %collective-permute-done.27 = bf16[2,256,256]{2,1,0:T(8,128)(2,1)S(1)} collective-permute-done((bf16[2,256,256]{2,1,0:T(8,128)(2,1)}, bf16[2,256,256]{2,1,0:T(8,128)(2,1)S(1)}, u32[]{:S(2)}, u32[]{:S(2)}) %collective-permute-start.27) | collective-permute-done | bytes 262176 | tf_op jit(solution)/shard_map/ppermute | solution.py:200
  130.0 3.2 %collective-permute-start.32 = (bf16[2,256,256]{2,1,0:T(8,128)(2,1)S(1)}, bf16[2,256,256]{2,1,0:T(8,128)(2,1)S(1)}, u32[]{:S(2)}, u32[]{:S(2)}) collective-permute-start(bf16[2,256,256]{2,1,0:T(8,128)(2,1)S(1)} %pad_maximum_fusion.3), channel_id=1, source_target_pairs={{0,24},{1,25},{2,26},{3,27},{4,28},{5,29},{6,30},{7,31},{8,0},{9,1... | collective-permute-start | bytes 786440 | tf_op jit(solution)/shard_map/ppermute | solution.py:200
  136.4 7.5 %collective-permute-done.31 = bf16[2,256,256]{2,1,0:T(8,128)(2,1)S(1)} collective-permute-done((bf16[2,256,256]{2,1,0:T(8,128)(2,1)S(1)}, bf16[2,256,256]{2,1,0:T(8,128)(2,1)S(1)}, u32[]{:S(2)}, u32[]{:S(2)}) %collective-permute-start.31) | collective-permute-done | bytes 262176 | tf_op jit(solution)/shard_map/ppermute | solution.py:200
  147.5 4.2 %collective-permute-done.30 = bf16[2,256,256]{2,1,0:T(8,128)(2,1)S(1)} collective-permute-done((bf16[2,256,256]{2,1,0:T(8,128)(2,1)S(1)}, bf16[2,256,256]{2,1,0:T(8,128)(2,1)S(1)}, u32[]{:S(2)}, u32[]{:S(2)}) %collective-permute-start.30) | collective-permute-done | bytes 262176 | tf_op jit(solution)/shard_map/ppermute | solution.py:200
  152.5 3.2 %collective-permute-start.35 = (bf16[8,256,256]{2,1,0:T(8,128)(2,1)}, bf16[8,256,256]{2,1,0:T(8,128)(2,1)S(1)}, u32[]{:S(2)}, u32[]{:S(2)}) collective-permute-start(bf16[8,256,256]{2,1,0:T(8,128)(2,1)} %constant_dynamic-update-slice_fusion.10.refs_3_), channel_id=1, source_target_pairs={{0,24},{1,25},{2,26},{3,27},{4,28},{5,29},{6,30},{7,31},{8,0},{9,1... | collective-permute-start | bytes 3145736 | tf_op jit(solution)/shard_map/ppermute | solution.py:200
  160.6 5.2 %shard_map.182.refs_14_ = f32[2,256,256]{2,1,0:T(8,128)} custom-call(s32[58]{0:T(128)} %get-tuple-element.68.refs_0_, s32[58]{0:T(128)} %get-tuple-element.67.refs_1_, s32[125]{0:T(128)} %convert_reduce_fusion.refs_2_, bf16[2,256,256]{2,1,0:T(8,128)(2,1)} %bitcast.39, bf16[8,256,256]{2,1,0:T(8,128)(2,1)} %constant_dynamic-update-slice_fusion.refs_4_, ...), custom_call_target="tpu_custom_call" | custom-call | flops 973078528 | bytes 7602176 | tf_op jit(solution)/shard_map/pallas_call | solution.py:95
  165.8 5.5 %shard_map.181.refs_14_ = f32[2,256,256]{2,1,0:T(8,128)} custom-call(s32[58]{0:T(128)} %get-tuple-element.68.refs_0_, s32[58]{0:T(128)} %get-tuple-element.67.refs_1_, s32[125]{0:T(128)} %convert_reduce_fusion.refs_2_, bf16[2,256,256]{2,1,0:T(8,128)(2,1)} %bitcast.40, bf16[8,256,256]{2,1,0:T(8,128)(2,1)} %constant_dynamic-update-slice_fusion.refs_4_, ...), custom_call_target="tpu_custom_call" | custom-call | flops 973078528 | bytes 7602176 | tf_op jit(solution)/shard_map/pallas_call | solution.py:95
  171.3 2.8 %collective-permute-done.34.refs_4_ = bf16[8,256,256]{2,1,0:T(8,128)(2,1)S(1)} collective-permute-done((bf16[8,256,256]{2,1,0:T(8,128)(2,1)}, bf16[8,256,256]{2,1,0:T(8,128)(2,1)S(1)}, u32[]{:S(2)}, u32[]{:S(2)}) %collective-permute-start.34) | collective-permute-done | bytes 1048608 | tf_op jit(solution)/shard_map/ppermute | solution.py:200
  175.6 3.3 %collective-permute-start.39 = (bf16[4,256,256]{2,1,0:T(8,128)(2,1)S(1)}, bf16[4,256,256]{2,1,0:T(8,128)(2,1)}, u32[]{:S(2)}, u32[]{:S(2)}) collective-permute-start(bf16[4,256,256]{2,1,0:T(8,128)(2,1)S(1)} %slice.61), channel_id=1, source_target_pairs={{0,24},{1,25},{2,26},{3,27},{4,28},{5,29},{6,30},{7,31},{8,0},{9,1... | collective-permute-start | bytes 1572872 | tf_op jit(solution)/shard_map/ppermute | solution.py:200
  178.9 2.4 %collective-permute-start.40 = (bf16[4,256,256]{2,1,0:T(8,128)(2,1)S(1)}, bf16[4,256,256]{2,1,0:T(8,128)(2,1)}, u32[]{:S(2)}, u32[]{:S(2)}) collective-permute-start(bf16[4,256,256]{2,1,0:T(8,128)(2,1)S(1)} %slice.62), channel_id=1, source_target_pairs={{0,2},{1,3},{2,4},{3,5},{4,6},{5,7},{6,0},{7,1},{8,10},{9,11},{10,... | collective-permute-start | bytes 1572872 | tf_op jit(solution)/shard_map/ppermute | solution.py:200
  183.1 2.8 %collective-permute-done.38.refs_6_ = bf16[4,256,256]{2,1,0:T(8,128)(2,1)S(1)} collective-permute-done((bf16[4,256,256]{2,1,0:T(8,128)(2,1)S(1)}, bf16[4,256,256]{2,1,0:T(8,128)(2,1)S(1)}, u32[]{:S(2)}, u32[]{:S(2)}) %collective-permute-start.38) | collective-permute-done | bytes 524320 | tf_op jit(solution)/shard_map/ppermute | solution.py:200
  185.9 3.3 %collective-permute-done.40.refs_11_ = bf16[4,256,256]{2,1,0:T(8,128)(2,1)} collective-permute-done((bf16[4,256,256]{2,1,0:T(8,128)(2,1)S(1)}, bf16[4,256,256]{2,1,0:T(8,128)(2,1)}, u32[]{:S(2)}, u32[]{:S(2)}) %collective-permute-start.40) | collective-permute-done | bytes 524320 | tf_op jit(solution)/shard_map/ppermute | solution.py:200
  189.2 3.4 %collective-permute-done.41.refs_12_ = bf16[4,256,256]{2,1,0:T(8,128)(2,1)} collective-permute-done((bf16[4,256,256]{2,1,0:T(8,128)(2,1)S(1)}, bf16[4,256,256]{2,1,0:T(8,128)(2,1)}, u32[]{:S(2)}, u32[]{:S(2)}) %collective-permute-start.41) | collective-permute-done | bytes 524320 | tf_op jit(solution)/shard_map/ppermute | solution.py:200
  192.7 4.3 %shard_map.184 = bf16[2,256,256]{2,1,0:T(8,128)(2,1)} custom-call(s32[58]{0:T(128)} %get-tuple-element.68.refs_0_, s32[58]{0:T(128)} %get-tuple-element.67.refs_1_, s32[125]{0:T(128)} %convert_reduce_fusion.refs_2_, bf16[8,256,256]{2,1,0:T(8,128)(2,1)} %constant_dynamic-update-slice_fusion.10.refs_3_, bf16[8,256,256]{2,1,0:T(8,128)(2,1)} %copy-done.10, ...), custom_call_target="tpu_custom_call" | custom-call | flops 973078528 | bytes 7602176 | tf_op jit(solution)/shard_map/pallas_call | solution.py:95
  199.2 4.4 %shard_map.183.mine = bf16[2,256,256]{2,1,0:T(8,128)(2,1)} custom-call(s32[58]{0:T(128)} %get-tuple-element.68.refs_0_, s32[58]{0:T(128)} %get-tuple-element.67.refs_1_, s32[125]{0:T(128)} %convert_reduce_fusion.refs_2_, bf16[8,256,256]{2,1,0:T(8,128)(2,1)} %constant_dynamic-update-slice_fusion.10.refs_3_, bf16[8,256,256]{2,1,0:T(8,128)(2,1)} %copy-done.10, ...), custom_call_target="tpu_custom_call" | custom-call | flops 973078528 | bytes 7602176 | tf_op jit(solution)/shard_map/pallas_call | solution.py:95
  205.9 2.4 %shard_map.185 = (f32[2,256,256]{2,1,0:T(8,128)}, bf16[2,256,256]{2,1,0:T(8,128)(2,1)}) custom-call(f32[2,256,256]{2,1,0:T(8,128)} %bitcast.43, bf16[2,256,256]{2,1,0:T(8,128)(2,1)} %shard_map.183.mine, bf16[2,256,256]{2,1,0:T(8,128)(2,1)} %copy-done.14, bf16[2,256,256]{2,1,0:T(8,128)(2,1)} %bitcast.46), custom_call_target="tpu_custom_call" | custom-call | tf_op jit(solution)/shard_map/pallas_call | solution.py:179
  (150 shorter events, 69.8 us)
Async XLA Ops:
  6.0 9.5 %collective-permute-start = (bf16[2,256,256]{2,1,0:T(8,128)(2,1)}, bf16[2,256,256]{2,1,0:T(8,128)(2,1)S(1)}, u32[]{:S(2)}, u32[]{:S(2)}) collective-permute-start(bf16[2,256,256]{2,1,0:T(8,128)(2,1)} %shard_map.176), channel_id=1, source_target_pairs={{0,32},{32,0},{1,33},{33,1},{2,34},{34,2},{3,35},{35,3},{4,36},{36... | collective-permute-start | bytes 786440 | tf_op jit(solution)/shard_map/ppermute | solution.py:188
  26.4 11.3 %collective-permute-start.5 = (bf16[2,256,256]{2,1,0:T(8,128)(2,1)S(1)}, bf16[2,256,256]{2,1,0:T(8,128)(2,1)S(1)}, u32[]{:S(2)}, u32[]{:S(2)}) collective-permute-start(bf16[2,256,256]{2,1,0:T(8,128)(2,1)S(1)} %pad_maximum_fusion.1), channel_id=1, source_target_pairs={{0,8},{1,9},{2,10},{3,11},{4,12},{5,13},{6,14},{7,15},{8,16},{9,17... | collective-permute-start | bytes 786440 | tf_op jit(solution)/shard_map/ppermute | solution.py:200
  28.7 12.5 %collective-permute-start.6 = (bf16[2,256,256]{2,1,0:T(8,128)(2,1)S(1)}, bf16[2,256,256]{2,1,0:T(8,128)(2,1)S(1)}, u32[]{:S(2)}, u32[]{:S(2)}) collective-permute-start(bf16[2,256,256]{2,1,0:T(8,128)(2,1)S(1)} %pad_maximum_fusion.1), channel_id=1, source_target_pairs={{0,24},{1,25},{2,26},{3,27},{4,28},{5,29},{6,30},{7,31},{8,0},{9,1... | collective-permute-start | bytes 786440 | tf_op jit(solution)/shard_map/ppermute | solution.py:200
  31.4 11.5 %collective-permute-start.7 = (bf16[2,256,256]{2,1,0:T(8,128)(2,1)S(1)}, bf16[2,256,256]{2,1,0:T(8,128)(2,1)S(1)}, u32[]{:S(2)}, u32[]{:S(2)}) collective-permute-start(bf16[2,256,256]{2,1,0:T(8,128)(2,1)S(1)} %pad_maximum_fusion.1), channel_id=1, source_target_pairs={{0,16},{1,17},{2,18},{3,19},{4,20},{5,21},{6,22},{7,23},{8,24},{9,... | collective-permute-start | bytes 786440 | tf_op jit(solution)/shard_map/ppermute | solution.py:200
  32.9 10.1 %collective-permute-start.2 = (bf16[2,256,256]{2,1,0:T(8,128)(2,1)S(1)}, bf16[2,256,256]{2,1,0:T(8,128)(2,1)S(1)}, u32[]{:S(2)}, u32[]{:S(2)}) collective-permute-start(bf16[2,256,256]{2,1,0:T(8,128)(2,1)S(1)} %pad_maximum_fusion), channel_id=1, source_target_pairs={{0,2},{1,3},{2,4},{3,5},{4,6},{5,7},{6,0},{7,1},{8,10},{9,11},{10,... | collective-permute-start | bytes 786440 | tf_op jit(solution)/shard_map/ppermute | solution.py:200
  34.7 9.1 %collective-permute-start.3 = (bf16[2,256,256]{2,1,0:T(8,128)(2,1)S(1)}, bf16[2,256,256]{2,1,0:T(8,128)(2,1)S(1)}, u32[]{:S(2)}, u32[]{:S(2)}) collective-permute-start(bf16[2,256,256]{2,1,0:T(8,128)(2,1)S(1)} %pad_maximum_fusion), channel_id=1, source_target_pairs={{0,6},{1,7},{2,0},{3,1},{4,2},{5,3},{6,4},{7,5},{8,14},{9,15},{10,... | collective-permute-start | bytes 786440 | tf_op jit(solution)/shard_map/ppermute | solution.py:200
  37.7 8.7 %collective-permute-start.4 = (bf16[2,256,256]{2,1,0:T(8,128)(2,1)S(1)}, bf16[2,256,256]{2,1,0:T(8,128)(2,1)S(1)}, u32[]{:S(2)}, u32[]{:S(2)}) collective-permute-start(bf16[2,256,256]{2,1,0:T(8,128)(2,1)S(1)} %pad_maximum_fusion), channel_id=1, source_target_pairs={{0,4},{1,5},{2,6},{3,7},{4,0},{5,1},{6,2},{7,3},{8,12},{9,13},{10,... | collective-permute-start | bytes 786440 | tf_op jit(solution)/shard_map/ppermute | solution.py:200
  47.1 21.5 %collective-permute-start.10 = (bf16[8,256,256]{2,1,0:T(8,128)(2,1)S(1)}, bf16[8,256,256]{2,1,0:T(8,128)(2,1)S(1)}, u32[]{:S(2)}, u32[]{:S(2)}) collective-permute-start(bf16[8,256,256]{2,1,0:T(8,128)(2,1)S(1)} %constant_dynamic-update-slice_fusion.5.refs_9_), channel_id=1, source_target_pairs={{0,2},{1,3},{2,4},{3,5},{4,6},{5,7},{6,0},{7,1},{8,10},{9,11},{10,... | collective-permute-start | bytes 3145736 | tf_op jit(solution)/shard_map/ppermute | solution.py:200
  47.5 21.7 %collective-permute-start.11 = (bf16[8,256,256]{2,1,0:T(8,128)(2,1)S(1)}, bf16[8,256,256]{2,1,0:T(8,128)(2,1)S(1)}, u32[]{:S(2)}, u32[]{:S(2)}) collective-permute-start(bf16[8,256,256]{2,1,0:T(8,128)(2,1)S(1)} %constant_dynamic-update-slice_fusion.5.refs_9_), channel_id=1, source_target_pairs={{0,6},{1,7},{2,0},{3,1},{4,2},{5,3},{6,4},{7,5},{8,14},{9,15},{10,... | collective-permute-start | bytes 3145736 | tf_op jit(solution)/shard_map/ppermute | solution.py:200
  49.1 23.4 %collective-permute-start.8 = (bf16[8,256,256]{2,1,0:T(8,128)(2,1)}, bf16[8,256,256]{2,1,0:T(8,128)(2,1)S(1)}, u32[]{:S(2)}, u32[]{:S(2)}) collective-permute-start(bf16[8,256,256]{2,1,0:T(8,128)(2,1)} %constant_dynamic-update-slice_fusion.refs_4_), channel_id=1, source_target_pairs={{0,8},{1,9},{2,10},{3,11},{4,12},{5,13},{6,14},{7,15},{8,16},{9,17... | collective-permute-start | bytes 3145736 | tf_op jit(solution)/shard_map/ppermute | solution.py:200
  52.6 20.0 %collective-permute-start.9 = (bf16[8,256,256]{2,1,0:T(8,128)(2,1)}, bf16[8,256,256]{2,1,0:T(8,128)(2,1)S(1)}, u32[]{:S(2)}, u32[]{:S(2)}) collective-permute-start(bf16[8,256,256]{2,1,0:T(8,128)(2,1)} %constant_dynamic-update-slice_fusion.refs_4_), channel_id=1, source_target_pairs={{0,24},{1,25},{2,26},{3,27},{4,28},{5,29},{6,30},{7,31},{8,0},{9,1... | collective-permute-start | bytes 3145736 | tf_op jit(solution)/shard_map/ppermute | solution.py:200
  72.6 10.6 %collective-permute-start.12 = (bf16[4,256,256]{2,1,0:T(8,128)(2,1)S(1)}, bf16[4,256,256]{2,1,0:T(8,128)(2,1)}, u32[]{:S(2)}, u32[]{:S(2)}) collective-permute-start(bf16[4,256,256]{2,1,0:T(8,128)(2,1)S(1)} %slice.52), channel_id=1, source_target_pairs={{0,8},{1,9},{2,10},{3,11},{4,12},{5,13},{6,14},{7,15},{8,16},{9,17... | collective-permute-start | bytes 1572872 | tf_op jit(solution)/shard_map/ppermute | solution.py:200
  73.7 9.5 %collective-permute-start.13 = (bf16[4,256,256]{2,1,0:T(8,128)(2,1)S(1)}, bf16[4,256,256]{2,1,0:T(8,128)(2,1)}, u32[]{:S(2)}, u32[]{:S(2)}) collective-permute-start(bf16[4,256,256]{2,1,0:T(8,128)(2,1)S(1)} %slice.53), channel_id=1, source_target_pairs={{0,24},{1,25},{2,26},{3,27},{4,28},{5,29},{6,30},{7,31},{8,0},{9,1... | collective-permute-start | bytes 1572872 | tf_op jit(solution)/shard_map/ppermute | solution.py:200
  76.2 9.4 %collective-permute-start.14 = (bf16[4,256,256]{2,1,0:T(8,128)(2,1)S(1)}, bf16[4,256,256]{2,1,0:T(8,128)(2,1)}, u32[]{:S(2)}, u32[]{:S(2)}) collective-permute-start(bf16[4,256,256]{2,1,0:T(8,128)(2,1)S(1)} %slice.54), channel_id=1, source_target_pairs={{0,2},{1,3},{2,4},{3,5},{4,6},{5,7},{6,0},{7,1},{8,10},{9,11},{10,... | collective-permute-start | bytes 1572872 | tf_op jit(solution)/shard_map/ppermute | solution.py:200
  77.7 9.4 %collective-permute-start.15 = (bf16[4,256,256]{2,1,0:T(8,128)(2,1)S(1)}, bf16[4,256,256]{2,1,0:T(8,128)(2,1)}, u32[]{:S(2)}, u32[]{:S(2)}) collective-permute-start(bf16[4,256,256]{2,1,0:T(8,128)(2,1)S(1)} %slice.55), channel_id=1, source_target_pairs={{0,6},{1,7},{2,0},{3,1},{4,2},{5,3},{6,4},{7,5},{8,14},{9,15},{10,... | collective-permute-start | bytes 1572872 | tf_op jit(solution)/shard_map/ppermute | solution.py:200
  107.4 10.5 %collective-permute-start.26 = (bf16[2,256,256]{2,1,0:T(8,128)(2,1)}, bf16[2,256,256]{2,1,0:T(8,128)(2,1)S(1)}, u32[]{:S(2)}, u32[]{:S(2)}) collective-permute-start(bf16[2,256,256]{2,1,0:T(8,128)(2,1)} %shard_map.179), channel_id=1, source_target_pairs={{0,32},{32,0},{1,33},{33,1},{2,34},{34,2},{3,35},{35,3},{4,36},{36... | collective-permute-start | bytes 786440 | tf_op jit(solution)/shard_map/ppermute | solution.py:188
  121.0 8.1 %collective-permute-start.27 = (bf16[2,256,256]{2,1,0:T(8,128)(2,1)}, bf16[2,256,256]{2,1,0:T(8,128)(2,1)S(1)}, u32[]{:S(2)}, u32[]{:S(2)}) collective-permute-start(bf16[2,256,256]{2,1,0:T(8,128)(2,1)} %get-tuple-element.57), channel_id=1, source_target_pairs={{0,1},{1,0},{2,3},{3,2},{4,5},{5,4},{6,7},{7,6},{8,9},{9,8},{10,11... | collective-permute-start | bytes 786440 | tf_op jit(solution)/shard_map/ppermute | solution.py:200
  129.9 13.9 %collective-permute-start.31 = (bf16[2,256,256]{2,1,0:T(8,128)(2,1)S(1)}, bf16[2,256,256]{2,1,0:T(8,128)(2,1)S(1)}, u32[]{:S(2)}, u32[]{:S(2)}) collective-permute-start(bf16[2,256,256]{2,1,0:T(8,128)(2,1)S(1)} %pad_maximum_fusion.3), channel_id=1, source_target_pairs={{0,8},{1,9},{2,10},{3,11},{4,12},{5,13},{6,14},{7,15},{8,16},{9,17... | collective-permute-start | bytes 786440 | tf_op jit(solution)/shard_map/ppermute | solution.py:200
  130.0 14.6 %collective-permute-start.32 = (bf16[2,256,256]{2,1,0:T(8,128)(2,1)S(1)}, bf16[2,256,256]{2,1,0:T(8,128)(2,1)S(1)}, u32[]{:S(2)}, u32[]{:S(2)}) collective-permute-start(bf16[2,256,256]{2,1,0:T(8,128)(2,1)S(1)} %pad_maximum_fusion.3), channel_id=1, source_target_pairs={{0,24},{1,25},{2,26},{3,27},{4,28},{5,29},{6,30},{7,31},{8,0},{9,1... | collective-permute-start | bytes 786440 | tf_op jit(solution)/shard_map/ppermute | solution.py:200
  133.2 12.1 %collective-permute-start.33 = (bf16[2,256,256]{2,1,0:T(8,128)(2,1)S(1)}, bf16[2,256,256]{2,1,0:T(8,128)(2,1)S(1)}, u32[]{:S(2)}, u32[]{:S(2)}) collective-permute-start(bf16[2,256,256]{2,1,0:T(8,128)(2,1)S(1)} %pad_maximum_fusion.3), channel_id=1, source_target_pairs={{0,16},{1,17},{2,18},{3,19},{4,20},{5,21},{6,22},{7,23},{8,24},{9,... | collective-permute-start | bytes 786440 | tf_op jit(solution)/shard_map/ppermute | solution.py:200
  133.3 12.8 %collective-permute-start.28 = (bf16[2,256,256]{2,1,0:T(8,128)(2,1)S(1)}, bf16[2,256,256]{2,1,0:T(8,128)(2,1)S(1)}, u32[]{:S(2)}, u32[]{:S(2)}) collective-permute-start(bf16[2,256,256]{2,1,0:T(8,128)(2,1)S(1)} %pad_maximum_fusion.2), channel_id=1, source_target_pairs={{0,2},{1,3},{2,4},{3,5},{4,6},{5,7},{6,0},{7,1},{8,10},{9,11},{10,... | collective-permute-start | bytes 786440 | tf_op jit(solution)/shard_map/ppermute | solution.py:200
  135.4 11.4 %collective-permute-start.29 = (bf16[2,256,256]{2,1,0:T(8,128)(2,1)S(1)}, bf16[2,256,256]{2,1,0:T(8,128)(2,1)S(1)}, u32[]{:S(2)}, u32[]{:S(2)}) collective-permute-start(bf16[2,256,256]{2,1,0:T(8,128)(2,1)S(1)} %pad_maximum_fusion.2), channel_id=1, source_target_pairs={{0,6},{1,7},{2,0},{3,1},{4,2},{5,3},{6,4},{7,5},{8,14},{9,15},{10,... | collective-permute-start | bytes 786440 | tf_op jit(solution)/shard_map/ppermute | solution.py:200
  143.9 7.9 %collective-permute-start.30 = (bf16[2,256,256]{2,1,0:T(8,128)(2,1)S(1)}, bf16[2,256,256]{2,1,0:T(8,128)(2,1)S(1)}, u32[]{:S(2)}, u32[]{:S(2)}) collective-permute-start(bf16[2,256,256]{2,1,0:T(8,128)(2,1)S(1)} %pad_maximum_fusion.2), channel_id=1, source_target_pairs={{0,4},{1,5},{2,6},{3,7},{4,0},{5,1},{6,2},{7,3},{8,12},{9,13},{10,... | collective-permute-start | bytes 786440 | tf_op jit(solution)/shard_map/ppermute | solution.py:200
  152.5 21.6 %collective-permute-start.34 = (bf16[8,256,256]{2,1,0:T(8,128)(2,1)}, bf16[8,256,256]{2,1,0:T(8,128)(2,1)S(1)}, u32[]{:S(2)}, u32[]{:S(2)}) collective-permute-start(bf16[8,256,256]{2,1,0:T(8,128)(2,1)} %constant_dynamic-update-slice_fusion.10.refs_3_), channel_id=1, source_target_pairs={{0,8},{1,9},{2,10},{3,11},{4,12},{5,13},{6,14},{7,15},{8,16},{9,17... | collective-permute-start | bytes 3145736 | tf_op jit(solution)/shard_map/ppermute | solution.py:200
  152.5 21.6 %collective-permute-start.35 = (bf16[8,256,256]{2,1,0:T(8,128)(2,1)}, bf16[8,256,256]{2,1,0:T(8,128)(2,1)S(1)}, u32[]{:S(2)}, u32[]{:S(2)}) collective-permute-start(bf16[8,256,256]{2,1,0:T(8,128)(2,1)} %constant_dynamic-update-slice_fusion.10.refs_3_), channel_id=1, source_target_pairs={{0,24},{1,25},{2,26},{3,27},{4,28},{5,29},{6,30},{7,31},{8,0},{9,1... | collective-permute-start | bytes 3145736 | tf_op jit(solution)/shard_map/ppermute | solution.py:200
  155.7 19.5 %collective-permute-start.36 = (bf16[8,256,256]{2,1,0:T(8,128)(2,1)}, bf16[8,256,256]{2,1,0:T(8,128)(2,1)S(1)}, u32[]{:S(2)}, u32[]{:S(2)}) collective-permute-start(bf16[8,256,256]{2,1,0:T(8,128)(2,1)} %constant_dynamic-update-slice_fusion.15.refs_8_), channel_id=1, source_target_pairs={{0,2},{1,3},{2,4},{3,5},{4,6},{5,7},{6,0},{7,1},{8,10},{9,11},{10,... | collective-permute-start | bytes 3145736 | tf_op jit(solution)/shard_map/ppermute | solution.py:200
  155.8 19.6 %collective-permute-start.37 = (bf16[8,256,256]{2,1,0:T(8,128)(2,1)}, bf16[8,256,256]{2,1,0:T(8,128)(2,1)}, u32[]{:S(2)}, u32[]{:S(2)}) collective-permute-start(bf16[8,256,256]{2,1,0:T(8,128)(2,1)} %constant_dynamic-update-slice_fusion.15.refs_8_), channel_id=1, source_target_pairs={{0,6},{1,7},{2,0},{3,1},{4,2},{5,3},{6,4},{7,5},{8,14},{9,15},{10,... | collective-permute-start | bytes 3145736 | tf_op jit(solution)/shard_map/ppermute | solution.py:200
  175.4 10.5 %collective-permute-start.38 = (bf16[4,256,256]{2,1,0:T(8,128)(2,1)S(1)}, bf16[4,256,256]{2,1,0:T(8,128)(2,1)S(1)}, u32[]{:S(2)}, u32[]{:S(2)}) collective-permute-start(bf16[4,256,256]{2,1,0:T(8,128)(2,1)S(1)} %slice.60), channel_id=1, source_target_pairs={{0,8},{1,9},{2,10},{3,11},{4,12},{5,13},{6,14},{7,15},{8,16},{9,17... | collective-permute-start | bytes 1572872 | tf_op jit(solution)/shard_map/ppermute | solution.py:200
  175.6 10.3 %collective-permute-start.39 = (bf16[4,256,256]{2,1,0:T(8,128)(2,1)S(1)}, bf16[4,256,256]{2,1,0:T(8,128)(2,1)}, u32[]{:S(2)}, u32[]{:S(2)}) collective-permute-start(bf16[4,256,256]{2,1,0:T(8,128)(2,1)S(1)} %slice.61), channel_id=1, source_target_pairs={{0,24},{1,25},{2,26},{3,27},{4,28},{5,29},{6,30},{7,31},{8,0},{9,1... | collective-permute-start | bytes 1572872 | tf_op jit(solution)/shard_map/ppermute | solution.py:200
  178.9 10.3 %collective-permute-start.40 = (bf16[4,256,256]{2,1,0:T(8,128)(2,1)S(1)}, bf16[4,256,256]{2,1,0:T(8,128)(2,1)}, u32[]{:S(2)}, u32[]{:S(2)}) collective-permute-start(bf16[4,256,256]{2,1,0:T(8,128)(2,1)S(1)} %slice.62), channel_id=1, source_target_pairs={{0,2},{1,3},{2,4},{3,5},{4,6},{5,7},{6,0},{7,1},{8,10},{9,11},{10,... | collective-permute-start | bytes 1572872 | tf_op jit(solution)/shard_map/ppermute | solution.py:200
  182.4 10.3 %collective-permute-start.41 = (bf16[4,256,256]{2,1,0:T(8,128)(2,1)S(1)}, bf16[4,256,256]{2,1,0:T(8,128)(2,1)}, u32[]{:S(2)}, u32[]{:S(2)}) collective-permute-start(bf16[4,256,256]{2,1,0:T(8,128)(2,1)S(1)} %slice.63), channel_id=1, source_target_pairs={{0,6},{1,7},{2,0},{3,1},{4,2},{5,3},{6,4},{7,5},{8,14},{9,15},{10,... | collective-permute-start | bytes 1572872 | tf_op jit(solution)/shard_map/ppermute | solution.py:200
  197.0 8.2 %collective-permute-start.42 = (bf16[2,256,256]{2,1,0:T(8,128)(2,1)}, bf16[2,256,256]{2,1,0:T(8,128)(2,1)S(1)}, u32[]{:S(2)}, u32[]{:S(2)}) collective-permute-start(bf16[2,256,256]{2,1,0:T(8,128)(2,1)} %shard_map.184), channel_id=1, source_target_pairs={{0,32},{32,0},{1,33},{33,1},{2,34},{34,2},{3,35},{35,3},{4,36},{36... | collective-permute-start | bytes 786440 | tf_op jit(solution)/shard_map/ppermute | solution.py:188
  (32 other events, 560.1 us)
